TPU v7x, 32 devices: a whole 2x2x4 slice. The times are simulated.
32 devices in a mesh: band: 4 (over x, core), pw: 8 (over z, y).
Axes of the slice: x: 2, y: 2, z: 4, core: 2. Of those that a mesh axis runs over, the one named last changes fastest.
Arguments:
- band_coeffs: bfloat16 [4, 2, 1024, 256], P('band', None, 'pw'), may hold values from -6 to 6
- potential: bfloat16 [8, 512, 512], P('pw'), may hold values from -6 to 6
- stick_list: int32 [1024, 2], replicated, may hold values from 1 to 255, as said below
Outputs:
- applied: bfloat16 [4, 2, 1024, 256], P('band', None, 'pw')
- correlation: float32 [2, 4, 4], P(None, None, 'band')
Inputs may be any that keep to these rules, and one draw needn't show every extreme that they name: `stick_list`: the rows are distinct box columns (x, y), each with (x - 128)^2 + (y - 128)^2 < 128^2.
All inputs are finite; a program needn't handle non-finite values.
Results may differ from a plain program's by a relative error of at most 0.019.
Values may be sent and summed in bfloat16 or wider, within the bound.
No kernel may reach another device: no remote copies, remote signals or barrier semaphores. Data moves between devices by JAX's collectives and lax.ppermute only.
A program may use at most 64 MiB of HBM per device.

v0:
```python
import functools
import math

import jax
import jax.numpy as jnp
import numpy as np
from jax import lax
from jax.experimental import pallas as pl
from jax.experimental.pallas import tpu as pltpu
from jax.sharding import PartitionSpec as P

F32 = jnp.float32
BF16 = jnp.bfloat16


def phases(box_index, grid_index, period, factor):
    turns = box_index[:, None] * grid_index[None, :] % period
    angles = turns * (2.0 * math.pi / period)
    return np.cos(angles) * factor, np.sin(angles) * factor


def plane_tables(box_edge, grid_len):
    half = grid_len // 2
    mats = []
    for parity in range(2):
        cos, sin = phases(
            np.arange(parity, box_edge, 2) - box_edge // 2, np.arange(half), grid_len, 1.0 / math.sqrt(box_edge)
        )
        mats.append(np.block([[cos, sin], [-sin, cos]]))
    mats = np.stack(mats)
    return jnp.asarray(mats, BF16), jnp.asarray(mats.transpose(0, 2, 1), BF16)


def z_tables(box_edge, slab_len, grid_len):
    cos, sin = phases(np.arange(box_edge) - box_edge // 2, np.arange(slab_len), grid_len, 1.0)
    inverse = np.concatenate([cos.T, sin.T]) / math.sqrt(box_edge)
    forward = np.block([[cos.T, -sin.T], [sin.T, cos.T]]) / math.sqrt(slab_len)
    return jnp.asarray(inverse, BF16), jnp.asarray(forward, BF16)


def dot_nt(left, right):
    return lax.dot_general(left, right, (((1,), (1,)), ((), ())), preferred_element_type=F32)


def dot_tn(left, right):
    return lax.dot_general(left, right, (((0,), (0,)), ((), ())), preferred_element_type=F32)


def dot_nn(left, right):
    return jnp.dot(left, right, preferred_element_type=F32)


def own_sphere(sticks_ref, stick_dev, box_edge):
    middle = box_edge // 2
    start = pl.multiple_of(lax.axis_index("pw") * stick_dev, stick_dev)
    own = sticks_ref[:, pl.ds(start, stick_dev)] - middle
    own = (own * own).astype(F32)
    radial = own[0:1] + own[1:2]
    column = jnp.broadcast_to(radial, (8, stick_dev)).T[:, 0:1]
    level = lax.broadcasted_iota(jnp.int32, (1, box_edge), 1) - middle
    return column + (level * level).astype(F32) < float(middle * middle)


def head_kernel(bands, coeffs_ref, sticks_ref, table_ref, out_ref):
    _, stick_dev, box_edge = coeffs_ref.shape
    slab_len = table_ref.shape[0] // 2
    sphere = own_sphere(sticks_ref, stick_dev, box_edge)
    table = table_ref[...]
    parts = []
    for c in range(2):
        masked = jnp.where(sphere, coeffs_ref[c].astype(F32), 0.0).astype(BF16)
        parts.append(dot_nt(table, masked))
    real = parts[0][:slab_len] - parts[1][slab_len:]
    imag = parts[0][slab_len:] + parts[1][:slab_len]
    real = real.astype(BF16).astype(F32)
    imag = imag.astype(BF16).astype(F32)
    for z in range(slab_len):
        row = jnp.concatenate([real[z : z + 1], imag[z : z + 1]], axis=0)
        for b in range(bands):
            out_ref[b * slab_len + z] = row


def plane_kernel(
    bands, recv_ref, pot_ref, sticks_ref, fwd_ref, tr_ref, out_ref, hot_a, hot_b, spread, half_ref, mid_ref, cell_ref, zeds
):
    box_edge = hot_a.shape[0]
    side = box_edge // 2
    sticks = sticks_ref.shape[1]
    groups = out_ref.shape[0]
    per = sticks // groups
    grid_len = pot_ref.shape[0]
    n_half = grid_len // 2

    codes = sticks_ref[...]
    codes = (codes & 1) * side + (codes >> 1)
    band = lax.axis_index("band")
    for g in range(groups):
        cols = slice(g * per, (g + 1) * per)
        rows = lax.broadcasted_iota(jnp.int32, (box_edge, per), 0)
        in_a = rows == codes[0:1, cols]
        in_b = rows == codes[1:2, cols]
        hot_a[:, cols] = jnp.where(in_a, 1.0, 0.0).astype(BF16)
        hot_b[:, cols] = jnp.where(in_b, 1.0, 0.0).astype(BF16)
        own = recv_ref[band * groups + g]
        for c in range(2):
            placed = jnp.where(in_b, own[c : c + 1], 0.0).astype(BF16)
            for p in range(2):
                at = p * box_edge + c * side
                spread[at : at + side, cols] = placed[p * side : (p + 1) * side]
        for i in range(bands):
            zeds[i : i + 1, cols] = recv_ref[i * groups + g, 0:1].astype(BF16)
            zeds[bands + i : bands + i + 1, cols] = recv_ref[i * groups + g, 1:2].astype(BF16)

    box = dot_nt(hot_a[...], spread[...]).astype(BF16)
    even = dot_nn(box[:, :box_edge], fwd_ref[0])
    odd = dot_nn(box[:, box_edge:], fwd_ref[1])
    low = (even + odd).astype(BF16)
    high = (even - odd).astype(BF16)
    for p in range(2):
        rows = slice(p * side, (p + 1) * side)
        for c in range(2):
            cols = slice(c * n_half, (c + 1) * n_half)
            half_ref[p, c * side : (c + 1) * side, :n_half] = low[rows, cols]
            half_ref[p, c * side : (c + 1) * side, n_half:] = high[rows, cols]

    step = 128
    for x0 in range(0, n_half, step):
        sums = {}
        for c in range(2):
            rows = slice(c * n_half + x0, c * n_half + x0 + step)
            even = dot_nn(tr_ref[0, rows], half_ref[0])
            odd = dot_nn(tr_ref[1, rows], half_ref[1])
            near = (even + odd) * pot_ref[x0 : x0 + step].astype(F32)
            far = (even - odd) * pot_ref[n_half + x0 : n_half + x0 + step].astype(F32)
            for p, both in ((0, near + far), (1, near - far)):
                sums[p, 0, c] = (both[:, :n_half] + both[:, n_half:]).astype(BF16)
                sums[p, 1, c] = (both[:, :n_half] - both[:, n_half:]).astype(BF16)
        for p in range(2):
            for q in range(2):
                left = jnp.concatenate([sums[p, q, 0], sums[p, q, 1]], axis=1)
                mid = dot_nn(left, tr_ref[q]).astype(BF16)
                for c in range(2):
                    mid_ref[p, c * n_half + x0 : c * n_half + x0 + step, q * side : (q + 1) * side] = mid[
                        :, c * side : (c + 1) * side
                    ]

    for p in range(2):
        cell = dot_nn(fwd_ref[p], mid_ref[p]) * (float(box_edge) / float(grid_len))
        cell_ref[p * box_edge : (p + 1) * box_edge] = cell.astype(BF16)

    wide = 256
    total = None
    for s0 in range(0, sticks, wide):
        cols = slice(s0, s0 + wide)
        picked = dot_nn(cell_ref[...], hot_b[:, cols])
        backs = []
        for c in range(2):
            value = None
            for p in range(2):
                at = p * box_edge + c * side
                term = jnp.sum(
                    picked[at : at + side] * hot_a[p * side : (p + 1) * side, cols].astype(F32), axis=0, keepdims=True
                )
                value = term if value is None else value + term
            backs.append(value)
        back = jnp.concatenate(backs, axis=0).astype(BF16)
        term = dot_nt(back, zeds[:, cols])
        total = term if total is None else total + term
        back = back.astype(F32)
        for g in range(s0 // per, (s0 + wide) // per):
            out_ref[g, 0:2] = back[:, g * per - s0 : (g + 1) * per - s0]
    for g in range(groups):
        out_ref[g, 2:4, : 2 * bands] = total
        out_ref[g, 2:4, 2 * bands :] = jnp.zeros((2, per - 2 * bands), F32)


def tail_kernel(bands, scale, recv_ref, sticks_ref, table_ref, out_ref, corr_ref):
    groups, _, stick_dev = recv_ref.shape
    box_edge = out_ref.shape[2]
    sphere = own_sphere(sticks_ref, stick_dev, box_edge)
    back = jnp.concatenate([recv_ref[:, 0], recv_ref[:, 1]], axis=0).astype(BF16)
    values = dot_tn(back, table_ref[...])
    for c in range(2):
        out_ref[c] = jnp.where(sphere, values[:, c * box_edge : (c + 1) * box_edge], 0.0).astype(BF16)
    total = recv_ref[0, 2:4]
    for g in range(1, groups):
        total = total + recv_ref[g, 2:4]
    real_row = total[0:1] * scale
    imag_row = total[1:2] * scale
    corr_ref[0] = real_row[:, :bands] + imag_row[:, bands : 2 * bands]
    corr_ref[1] = imag_row[:, :bands] - real_row[:, bands : 2 * bands]


def local(band_coeffs, potential, stick_list):
    groups = lax.axis_size("pw")
    bands = lax.axis_size("band") * band_coeffs.shape[0]
    _, _, stick_dev, box_edge = band_coeffs.shape
    grid_len = potential.shape[1]
    slab_len = potential.shape[0] * groups
    sticks = stick_list.shape[0]
    columns = stick_list.T
    fwd, transposed = plane_tables(box_edge, grid_len)
    z_inverse, z_forward = z_tables(box_edge, slab_len, grid_len)

    send = pl.pallas_call(
        functools.partial(head_kernel, bands),
        out_shape=jax.ShapeDtypeStruct((bands * groups, 2, stick_dev), F32),
        compiler_params=pltpu.CompilerParams(vmem_limit_bytes=4 << 20),
        name="head",
    )(band_coeffs[0], columns, z_inverse)
    planes = lax.all_to_all(send, ("band", "pw"), split_axis=0, concat_axis=0, tiled=True)
    backs = pl.pallas_call(
        functools.partial(plane_kernel, bands),
        out_shape=jax.ShapeDtypeStruct((groups, 4, stick_dev), F32),
        scratch_shapes=[
            pltpu.VMEM((box_edge, sticks), BF16),
            pltpu.VMEM((box_edge, sticks), BF16),
            pltpu.VMEM((2 * box_edge, sticks), BF16),
            pltpu.VMEM((2, box_edge, grid_len), BF16),
            pltpu.VMEM((2, grid_len, box_edge), BF16),
            pltpu.VMEM((2 * box_edge, box_edge), BF16),
            pltpu.VMEM((2 * bands, sticks), BF16),
        ],
        compiler_params=pltpu.CompilerParams(vmem_limit_bytes=32 << 20),
        name="plane",
    )(planes, potential[0], columns, fwd, transposed)
    back = lax.all_to_all(backs, "pw", split_axis=0, concat_axis=0, tiled=True)
    applied, correlation = pl.pallas_call(
        functools.partial(tail_kernel, bands, 1.0 / math.sqrt(slab_len * sticks)),
        out_shape=[
            jax.ShapeDtypeStruct((2, stick_dev, box_edge), BF16),
            jax.ShapeDtypeStruct((2, 1, bands), F32),
        ],
        compiler_params=pltpu.CompilerParams(vmem_limit_bytes=4 << 20),
        name="tail",
    )(back, columns, z_forward)
    return applied[None], correlation.transpose(0, 2, 1)


def solution(mesh):
    return jax.shard_map(
        local,
        mesh=mesh,
        in_specs=(P("band", None, "pw", None), P("pw", None, None), P()),
        out_specs=(P("band", None, "pw", None), P(None, None, "band")),
        check_vma=False,
    )
```

profile of v0, /device:TPU:0, one launch (start us, length us, event | category | flops | bytes accessed | tf_op | source)
XLA Modules:
  0.0 33.7 jit_solution(14825532726625460330)
XLA Ops:
  0.6 0.0 copy-start.7
  0.6 0.7 %copy-done.7 = bf16[16,256]{1,0:T(8,128)(2,1)S(1)} copy-done((bf16[16,256]{1,0:T(8,128)(2,1)S(1)}, bf16[16,256]{1,0:T(8,128)(2,1)}, u32[]{:S(2)}) %copy-start.7) | copy-done | bytes 8216
  1.3 0.0 copy-start.3
  1.3 0.9 %copy-done.3 = bf16[1,2,128,256]{3,2,1,0:T(8,128)(2,1)S(1)} copy-done((bf16[1,2,128,256]{3,2,1,0:T(8,128)(2,1)S(1)}, bf16[1,2,128,256]{3,2,1,0:T(8,128)(2,1)}, u32[]{:S(2)}) %copy-start.3) | copy-done | bytes 131096
  2.2 0.0 copy-start.4
  2.2 0.7 %copy-done.4 = s32[1024,2]{0,1:T(2,128)S(1)} copy-done((s32[1024,2]{0,1:T(2,128)S(1)}, s32[1024,2]{0,1:T(2,128)}, u32[]{:S(2)}) %copy-start.4) | copy-done | bytes 8216
  2.9 0.3 head.1
  3.2 0.0 copy-start.5
  3.3 14.3 %all_to_all.10.recv_ref = f32[32,2,128]{2,1,0:T(2,128)S(1)} all-to-all(f32[32,2,128]{2,1,0:T(2,128)S(1)} %head.1), channel_id=1, replica_groups=mesh['band'=4,'pw'=8] {'band','pw'}, dimensions={0} | all-to-all | bytes 65536 | tf_op jit(solution)/shard_map/all_to_all | solution.py:211
  17.5 0.0 copy-done.5
  17.6 0.0 copy-start
  17.6 1.0 %copy-done = bf16[1,512,512]{2,1,0:T(8,128)(2,1)S(1)} copy-done((bf16[1,512,512]{2,1,0:T(8,128)(2,1)S(1)}, bf16[1,512,512]{2,1,0:T(8,128)(2,1)}, u32[]{:S(2)}) %copy-start) | copy-done | bytes 524312
  18.6 0.0 copy-start.1
  18.6 1.0 %copy-done.1 = bf16[2,512,256]{2,1,0:T(8,128)(2,1)S(1)} copy-done((bf16[2,512,256]{2,1,0:T(8,128)(2,1)S(1)}, bf16[2,512,256]{2,1,0:T(8,128)(2,1)}, u32[]{:S(2)}) %copy-start.1) | copy-done | bytes 524312
  19.6 0.0 copy-start.2
  19.6 1.0 %copy-done.2 = bf16[2,256,512]{2,1,0:T(8,128)(2,1)S(1)} copy-done((bf16[2,256,512]{2,1,0:T(8,128)(2,1)S(1)}, bf16[2,256,512]{2,1,0:T(8,128)(2,1)}, u32[]{:S(2)}) %copy-start.2) | copy-done | bytes 524312
  20.7 3.0 %plane.1 = f32[8,4,128]{2,1,0:T(4,128)S(1)} custom-call(f32[32,2,128]{2,1,0:T(2,128)S(1)} %all_to_all.10.recv_ref, bf16[512,512]{1,0:T(8,128)(2,1)S(1)} %bitcast.7, s32[2,1024]{1,0:T(2,128)S(1)} %bitcast.10, bf16[2,256,512]{2,1,0:T(8,128)(2,1)S(1)} %copy-done.2, bf16[2,512,256]{2,1,0:T(8,128)(2,1)S(1)} %copy-done.1), custom_call_target="tpu_custom_call" | custom-call | tf_op jit(solution)/shard_map/plane/pallas_call | solution.py:212
  23.7 0.0 copy-start.6
  23.7 9.1 %all_to_all.11.recv_ref = f32[8,4,128]{2,1,0:T(4,128)S(1)} all-to-all(f32[8,4,128]{2,1,0:T(4,128)S(1)} %plane.1), channel_id=1, replica_groups=mesh['band'=4,'pw'=8] {'pw'}, dimensions={0} | all-to-all | bytes 32768 | tf_op jit(solution)/shard_map/all_to_all | solution.py:227
  32.8 0.0 copy-done.6
  32.8 0.9 %tail.1 = (bf16[2,128,256]{2,1,0:T(8,128)(2,1)}, f32[2,1,4]{2,1,0:T(1,128)}) custom-call(f32[8,4,128]{2,1,0:T(4,128)S(1)} %all_to_all.11.recv_ref, s32[2,1024]{1,0:T(2,128)S(1)} %bitcast.11, bf16[16,512]{1,0:T(8,128)(2,1)S(1)} %copy-done.6), custom_call_target="tpu_custom_call" | custom-call | tf_op jit(solution)/shard_map/tail/pallas_call | solution.py:228
Async XLA Ops:
  0.6 0.7 %copy-start.7 = (bf16[16,256]{1,0:T(8,128)(2,1)S(1)}, bf16[16,256]{1,0:T(8,128)(2,1)}, u32[]{:S(2)}) copy-start(bf16[16,256]{1,0:T(8,128)(2,1)} %constant.10.clone.table_ref) | copy-start | bytes 24580
  1.3 0.9 %copy-start.3 = (bf16[1,2,128,256]{3,2,1,0:T(8,128)(2,1)S(1)}, bf16[1,2,128,256]{3,2,1,0:T(8,128)(2,1)}, u32[]{:S(2)}) copy-start(bf16[1,2,128,256]{3,2,1,0:T(8,128)(2,1)} %param.7) | copy-start | bytes 393220
  2.2 0.7 %copy-start.4 = (s32[1024,2]{0,1:T(2,128)S(1)}, s32[1024,2]{0,1:T(2,128)}, u32[]{:S(2)}) copy-start(s32[1024,2]{0,1:T(2,128)} %param.9) | copy-start | bytes 24580
  3.2 14.3 %copy-start.5 = (s32[1024,2]{0,1:T(2,128)S(1)}, s32[1024,2]{0,1:T(2,128)}, u32[]{:S(2)}) copy-start(s32[1024,2]{0,1:T(2,128)} %param.9) | copy-start | bytes 24580
  17.6 1.0 %copy-start = (bf16[1,512,512]{2,1,0:T(8,128)(2,1)S(1)}, bf16[1,512,512]{2,1,0:T(8,128)(2,1)}, u32[]{:S(2)}) copy-start(bf16[1,512,512]{2,1,0:T(8,128)(2,1)} %param.8) | copy-start | bytes 1572868
  18.6 1.0 %copy-start.1 = (bf16[2,512,256]{2,1,0:T(8,128)(2,1)S(1)}, bf16[2,512,256]{2,1,0:T(8,128)(2,1)}, u32[]{:S(2)}) copy-start(bf16[2,512,256]{2,1,0:T(8,128)(2,1)} %constant.9.clone.tr_ref) | copy-start | bytes 1572868
  19.6 1.0 %copy-start.2 = (bf16[2,256,512]{2,1,0:T(8,128)(2,1)S(1)}, bf16[2,256,512]{2,1,0:T(8,128)(2,1)}, u32[]{:S(2)}) copy-start(bf16[2,256,512]{2,1,0:T(8,128)(2,1)} %constant.8.clone.fwd_ref) | copy-start | bytes 1572868
  23.7 9.1 %copy-start.6 = (bf16[16,512]{1,0:T(8,128)(2,1)S(1)}, bf16[16,512]{1,0:T(8,128)(2,1)}, u32[]{:S(2)}) copy-start(bf16[16,512]{1,0:T(8,128)(2,1)} %constant.11.clone.table_ref) | copy-start | bytes 49156
where the time goes:
time: 34.2 us; the launch traced here: 33.7 us
  blocking collectives  23.4 us (68%)
  local copies, waits for them, and re-layouts  5.43 us (16%)
  Pallas kernels  4.24 us (12%)
  between operations  0.66 us (2%)
    all_to_all x1, blocking collectives, local(): lax.all_to_all(send, ('band', 'pw'), split_axis=0, concat_axis=0, tiled=T...  14.3 us
    all_to_all x1, blocking collectives, local(): back = lax.all_to_all(backs, 'pw', split_axis=0, concat_axis=0, tiled=True)  9.07 us
    unnamed x16, local copies, waits for them, and re-layouts  5.43 us
    pallas_call x1, Pallas kernels, local(): pl.pallas_call(functools.partial(plane_kernel, bands), out_shape=jax.Shap...  3.03 us
    pallas_call x1, Pallas kernels, local(): pl.pallas_call(functools.partial(tail_kernel, bands, 1.0 / math.sqrt(slab...  0.9 us

commit v1 on v0

--- a/solution.py
+++ b/solution.py
@@ -61,10 +61,20 @@
     return column + (level * level).astype(F32) < float(middle * middle)
 
 
-def head_kernel(bands, coeffs_ref, sticks_ref, table_ref, out_ref):
+def head_kernel(bands, coeffs_hbm, sticks_hbm, table_hbm, out_ref, coeffs_ref, sticks_ref, table_ref, sems):
+    copies = [
+        pltpu.make_async_copy(sticks_hbm, sticks_ref, sems.at[0]),
+        pltpu.make_async_copy(coeffs_hbm, coeffs_ref, sems.at[1]),
+        pltpu.make_async_copy(table_hbm, table_ref, sems.at[2]),
+    ]
+    for copy in copies:
+        copy.start()
     _, stick_dev, box_edge = coeffs_ref.shape
+    copies[0].wait()
     slab_len = table_ref.shape[0] // 2
     sphere = own_sphere(sticks_ref, stick_dev, box_edge)
+    copies[1].wait()
+    copies[2].wait()
     table = table_ref[...]
     parts = []
     for c in range(2):
@@ -81,8 +91,32 @@
 
 
 def plane_kernel(
-    bands, recv_ref, pot_ref, sticks_ref, fwd_ref, tr_ref, out_ref, hot_a, hot_b, spread, half_ref, mid_ref, cell_ref, zeds
+    bands,
+    recv_ref,
+    sticks_ref,
+    pot_hbm,
+    fwd_hbm,
+    tr_hbm,
+    out_ref,
+    pot_ref,
+    fwd_ref,
+    tr_ref,
+    hot_a,
+    hot_b,
+    spread,
+    half_ref,
+    mid_ref,
+    cell_ref,
+    zeds,
+    sems,
 ):
+    copies = [
+        pltpu.make_async_copy(fwd_hbm, fwd_ref, sems.at[0]),
+        pltpu.make_async_copy(tr_hbm, tr_ref, sems.at[1]),
+        pltpu.make_async_copy(pot_hbm, pot_ref, sems.at[2]),
+    ]
+    for copy in copies:
+        copy.start()
     box_edge = hot_a.shape[0]
     side = box_edge // 2
     sticks = sticks_ref.shape[1]
@@ -112,6 +146,7 @@
             zeds[bands + i : bands + i + 1, cols] = recv_ref[i * groups + g, 1:2].astype(BF16)
 
     box = dot_nt(hot_a[...], spread[...]).astype(BF16)
+    copies[0].wait()
     even = dot_nn(box[:, :box_edge], fwd_ref[0])
     odd = dot_nn(box[:, box_edge:], fwd_ref[1])
     low = (even + odd).astype(BF16)
@@ -123,6 +158,8 @@
             half_ref[p, c * side : (c + 1) * side, :n_half] = low[rows, cols]
             half_ref[p, c * side : (c + 1) * side, n_half:] = high[rows, cols]
 
+    copies[1].wait()
+    copies[2].wait()
     step = 128
     for x0 in range(0, n_half, step):
         sums = {}
@@ -201,18 +238,30 @@
     columns = stick_list.T
     fwd, transposed = plane_tables(box_edge, grid_len)
     z_inverse, z_forward = z_tables(box_edge, slab_len, grid_len)
+    in_hbm = functools.partial(pltpu.with_memory_space_constraint, memory_space=pltpu.HBM)
 
     send = pl.pallas_call(
         functools.partial(head_kernel, bands),
         out_shape=jax.ShapeDtypeStruct((bands * groups, 2, stick_dev), F32),
+        in_specs=[pl.BlockSpec(memory_space=pltpu.HBM)] * 3,
+        scratch_shapes=[
+            pltpu.VMEM((2, stick_dev, box_edge), BF16),
+            pltpu.VMEM((2, sticks), jnp.int32),
+            pltpu.VMEM(z_inverse.shape, BF16),
+            pltpu.SemaphoreType.DMA((3,)),
+        ],
         compiler_params=pltpu.CompilerParams(vmem_limit_bytes=4 << 20),
         name="head",
-    )(band_coeffs[0], columns, z_inverse)
+    )(in_hbm(band_coeffs[0]), in_hbm(columns), in_hbm(z_inverse))
     planes = lax.all_to_all(send, ("band", "pw"), split_axis=0, concat_axis=0, tiled=True)
     backs = pl.pallas_call(
         functools.partial(plane_kernel, bands),
         out_shape=jax.ShapeDtypeStruct((groups, 4, stick_dev), F32),
+        in_specs=[pl.BlockSpec(memory_space=pltpu.VMEM)] * 2 + [pl.BlockSpec(memory_space=pltpu.HBM)] * 3,
         scratch_shapes=[
+            pltpu.VMEM((grid_len, grid_len), BF16),
+            pltpu.VMEM(fwd.shape, BF16),
+            pltpu.VMEM(transposed.shape, BF16),
             pltpu.VMEM((box_edge, sticks), BF16),
             pltpu.VMEM((box_edge, sticks), BF16),
             pltpu.VMEM((2 * box_edge, sticks), BF16),
@@ -220,10 +269,11 @@
             pltpu.VMEM((2, grid_len, box_edge), BF16),
             pltpu.VMEM((2 * box_edge, box_edge), BF16),
             pltpu.VMEM((2 * bands, sticks), BF16),
+            pltpu.SemaphoreType.DMA((3,)),
         ],
         compiler_params=pltpu.CompilerParams(vmem_limit_bytes=32 << 20),
         name="plane",
-    )(planes, potential[0], columns, fwd, transposed)
+    )(planes, columns, in_hbm(potential[0]), in_hbm(fwd), in_hbm(transposed))
     back = lax.all_to_all(backs, "pw", split_axis=0, concat_axis=0, tiled=True)
     applied, correlation = pl.pallas_call(
         functools.partial(tail_kernel, bands, 1.0 / math.sqrt(slab_len * sticks)),

time: 34.2 us -> 30.2 us (0.88)
  local copies, waits for them, and re-layouts: 5.43 us -> 0.01 us
  Pallas kernels: 4.24 us -> 6.05 us
    unnamed x16 -> x4, local copies, waits for them, and re-layouts: 5.43 us -> 0.01 us
    pallas_call x1, Pallas kernels: 3.03 us -> 4.04 us  [local(): pl.pallas_call(functools.partial(plane_kernel, bands), out_shape=jax.Shap...]
    pallas_call x1, Pallas kernels: 0.31 us -> 1.11 us  [local(): pl.pallas_call(functools.partial(head_kernel, bands), out_shape=jax.Shape...]
where the time goes in v1:
time: 30.2 us; the launch traced here: 30 us
  blocking collectives  23.2 us (77%)
  Pallas kernels  6.05 us (20%)
  between operations  0.66 us (2%)
    all_to_all x1, blocking collectives, local(): lax.all_to_all(send, ('band', 'pw'), split_axis=0, concat_axis=0, tiled=T...  14.3 us
    all_to_all x1, blocking collectives, local(): back = lax.all_to_all(backs, 'pw', split_axis=0, concat_axis=0, tiled=True)  8.94 us
    pallas_call x1, Pallas kernels, local(): pl.pallas_call(functools.partial(plane_kernel, bands), out_shape=jax.Shap...  4.04 us
    pallas_call x1, Pallas kernels, local(): pl.pallas_call(functools.partial(head_kernel, bands), out_shape=jax.Shape...  1.11 us
    pallas_call x1, Pallas kernels, local(): pl.pallas_call(functools.partial(tail_kernel, bands, 1.0 / math.sqrt(slab...  0.9 us

profile of v1, /device:TPU:0, one launch (start us, length us, event | category | flops | bytes accessed | tf_op | source)
XLA Modules:
  0.0 30.0 jit_solution(6721711085028386085)
XLA Ops:
  0.6 1.1 %head.1 = f32[32,2,128]{2,1,0:T(2,128)S(1)} custom-call(bf16[2,128,256]{2,1,0:T(8,128)(2,1)} %bitcast.11, s32[2,1024]{1,0:T(2,128)} %bitcast.7, bf16[16,256]{1,0:T(8,128)(2,1)} %constant.10.clone.table_hbm), custom_call_target="tpu_custom_call" | custom-call | tf_op jit(solution)/shard_map/head/pallas_call | solution.py:243
  1.8 0.0 copy-start
  1.8 14.3 %all_to_all.10.recv_ref = f32[32,2,128]{2,1,0:T(2,128)S(1)} all-to-all(f32[32,2,128]{2,1,0:T(2,128)S(1)} %head.1), channel_id=1, replica_groups=mesh['band'=4,'pw'=8] {'band','pw'}, dimensions={0} | all-to-all | bytes 65536 | tf_op jit(solution)/shard_map/all_to_all | solution.py:256
  16.1 0.0 copy-done
  16.1 4.0 %plane.1 = f32[8,4,128]{2,1,0:T(4,128)S(1)} custom-call(f32[32,2,128]{2,1,0:T(2,128)S(1)} %all_to_all.10.recv_ref, s32[2,1024]{1,0:T(2,128)S(1)} %bitcast.8, bf16[512,512]{1,0:T(8,128)(2,1)} %bitcast.10, bf16[2,256,512]{2,1,0:T(8,128)(2,1)} %constant.8.clone.fwd_hbm, bf16[2,512,256]{2,1,0:T(8,128)(2,1)} %constant.9.clone.tr_hbm), custom_call_target="tpu_custom_call" | custom-call | tf_op jit(solution)/shard_map/plane/pallas_call | solution.py:257
  20.1 0.0 copy-start.1
  20.1 8.9 %all_to_all.11.recv_ref = f32[8,4,128]{2,1,0:T(4,128)S(1)} all-to-all(f32[8,4,128]{2,1,0:T(4,128)S(1)} %plane.1), channel_id=1, replica_groups=mesh['band'=4,'pw'=8] {'pw'}, dimensions={0} | all-to-all | bytes 32768 | tf_op jit(solution)/shard_map/all_to_all | solution.py:277
  29.1 0.0 copy-done.1
  29.1 0.9 %tail.1 = (bf16[2,128,256]{2,1,0:T(8,128)(2,1)}, f32[2,1,4]{2,1,0:T(1,128)}) custom-call(f32[8,4,128]{2,1,0:T(4,128)S(1)} %all_to_all.11.recv_ref, s32[2,1024]{1,0:T(2,128)S(1)} %bitcast.9, bf16[16,512]{1,0:T(8,128)(2,1)S(1)} %copy-done.1), custom_call_target="tpu_custom_call" | custom-call | tf_op jit(solution)/shard_map/tail/pallas_call | solution.py:278
Async XLA Ops:
  1.8 14.3 %copy-start = (s32[1024,2]{0,1:T(2,128)S(1)}, s32[1024,2]{0,1:T(2,128)}, u32[]{:S(2)}) copy-start(s32[1024,2]{0,1:T(2,128)} %param.9) | copy-start | bytes 24580
  20.1 9.0 %copy-start.1 = (bf16[16,512]{1,0:T(8,128)(2,1)S(1)}, bf16[16,512]{1,0:T(8,128)(2,1)}, u32[]{:S(2)}) copy-start(bf16[16,512]{1,0:T(8,128)(2,1)} %constant.11.clone.table_ref) | copy-start | bytes 49156

commit v2 on v0

--- a/solution.py
+++ b/solution.py
@@ -61,10 +61,43 @@
     return column + (level * level).astype(F32) < float(middle * middle)
 
 
-def head_kernel(bands, coeffs_ref, sticks_ref, table_ref, out_ref):
+def head_kernel(
+    mates,
+    coeffs_hbm,
+    sticks_hbm,
+    table_hbm,
+    pot_hbm,
+    fwd_hbm,
+    tr_hbm,
+    out_ref,
+    hot_a,
+    hot_b,
+    pot_ref,
+    fwd_ref,
+    tr_ref,
+    coeffs_ref,
+    sticks_ref,
+    table_ref,
+    sems,
+):
+    pairs = [
+        (sticks_hbm, sticks_ref),
+        (coeffs_hbm, coeffs_ref),
+        (table_hbm, table_ref),
+        (fwd_hbm, fwd_ref),
+        (tr_hbm, tr_ref),
+        (pot_hbm, pot_ref),
+    ]
+    copies = [pltpu.make_async_copy(src, dst, sems.at[n]) for n, (src, dst) in enumerate(pairs)]
+    for copy in copies:
+        copy.start()
     _, stick_dev, box_edge = coeffs_ref.shape
     slab_len = table_ref.shape[0] // 2
+    side = box_edge // 2
+    copies[0].wait()
     sphere = own_sphere(sticks_ref, stick_dev, box_edge)
+    copies[1].wait()
+    copies[2].wait()
     table = table_ref[...]
     parts = []
     for c in range(2):
@@ -76,40 +109,40 @@
     imag = imag.astype(BF16).astype(F32)
     for z in range(slab_len):
         row = jnp.concatenate([real[z : z + 1], imag[z : z + 1]], axis=0)
-        for b in range(bands):
-            out_ref[b * slab_len + z] = row
+        for b in range(mates):
+            out_ref[(slab_len - 1 - z) * mates + b] = row
+
+    codes = sticks_ref[...]
+    codes = (codes & 1) * side + (codes >> 1)
+    rows = lax.broadcasted_iota(jnp.int32, (box_edge, stick_dev), 0)
+    for at in range(0, codes.shape[1], stick_dev):
+        cols = slice(at, at + stick_dev)
+        hot_a[:, cols] = jnp.where(rows == codes[0:1, cols], 1.0, 0.0).astype(BF16)
+        hot_b[:, cols] = jnp.where(rows == codes[1:2, cols], 1.0, 0.0).astype(BF16)
+    for copy in copies[3:]:
+        copy.wait()
 
 
 def plane_kernel(
-    bands, recv_ref, pot_ref, sticks_ref, fwd_ref, tr_ref, out_ref, hot_a, hot_b, spread, half_ref, mid_ref, cell_ref, zeds
+    mates, recv_ref, hot_a, hot_b, pot_ref, fwd_ref, tr_ref, cell_ref, spread, half_ref, mid_ref
 ):
-    box_edge = hot_a.shape[0]
+    box_edge, sticks = hot_a.shape
     side = box_edge // 2
-    sticks = sticks_ref.shape[1]
-    groups = out_ref.shape[0]
+    groups = recv_ref.shape[0] // mates
     per = sticks // groups
     grid_len = pot_ref.shape[0]
     n_half = grid_len // 2
 
-    codes = sticks_ref[...]
-    codes = (codes & 1) * side + (codes >> 1)
-    band = lax.axis_index("band")
+    own_mate = lax.rem(lax.axis_index("band"), mates)
     for g in range(groups):
         cols = slice(g * per, (g + 1) * per)
-        rows = lax.broadcasted_iota(jnp.int32, (box_edge, per), 0)
-        in_a = rows == codes[0:1, cols]
-        in_b = rows == codes[1:2, cols]
-        hot_a[:, cols] = jnp.where(in_a, 1.0, 0.0).astype(BF16)
-        hot_b[:, cols] = jnp.where(in_b, 1.0, 0.0).astype(BF16)
-        own = recv_ref[band * groups + g]
+        at = (groups - 1 - g) * mates
+        own = recv_ref[at + own_mate].astype(BF16)
         for c in range(2):
-            placed = jnp.where(in_b, own[c : c + 1], 0.0).astype(BF16)
+            placed = hot_b[:, cols] * own[c : c + 1]
             for p in range(2):
-                at = p * box_edge + c * side
-                spread[at : at + side, cols] = placed[p * side : (p + 1) * side]
-        for i in range(bands):
-            zeds[i : i + 1, cols] = recv_ref[i * groups + g, 0:1].astype(BF16)
-            zeds[bands + i : bands + i + 1, cols] = recv_ref[i * groups + g, 1:2].astype(BF16)
+                row = p * box_edge + c * side
+                spread[row : row + side, cols] = placed[p * side : (p + 1) * side]
 
     box = dot_nt(hot_a[...], spread[...]).astype(BF16)
     even = dot_nn(box[:, :box_edge], fwd_ref[0])
@@ -148,52 +181,70 @@
         cell = dot_nn(fwd_ref[p], mid_ref[p]) * (float(box_edge) / float(grid_len))
         cell_ref[p * box_edge : (p + 1) * box_edge] = cell.astype(BF16)
 
+
+def read_kernel(mates, count, *refs):
+    cell_ref, hot_a, hot_b = refs[:3]
+    planes = refs[3 : 3 + count]
+    out_ref, all_zeds = refs[3 + count :]
+    box_edge, sticks = hot_a.shape
+    side = box_edge // 2
+    groups = out_ref.shape[0]
+    per = sticks // groups
+
+    backs = [[], []]
     wide = 256
-    total = None
     for s0 in range(0, sticks, wide):
         cols = slice(s0, s0 + wide)
         picked = dot_nn(cell_ref[...], hot_b[:, cols])
-        backs = []
         for c in range(2):
             value = None
             for p in range(2):
                 at = p * box_edge + c * side
-                term = jnp.sum(
-                    picked[at : at + side] * hot_a[p * side : (p + 1) * side, cols].astype(F32), axis=0, keepdims=True
-                )
+                term = picked[at : at + side] * hot_a[p * side : (p + 1) * side, cols].astype(F32)
                 value = term if value is None else value + term
-            backs.append(value)
-        back = jnp.concatenate(backs, axis=0).astype(BF16)
-        term = dot_nt(back, zeds[:, cols])
-        total = term if total is None else total + term
-        back = back.astype(F32)
-        for g in range(s0 // per, (s0 + wide) // per):
-            out_ref[g, 0:2] = back[:, g * per - s0 : (g + 1) * per - s0]
+            backs[c].append(jnp.sum(value, axis=0, keepdims=True))
+    back = jnp.concatenate([jnp.concatenate(parts, axis=1) for parts in backs], axis=0)
+
+    here = lax.axis_index("band") // mates
+    for s in range(count):
+        source = lax.rem(here - s + count, count)
+        all_zeds[source, 2 * mates :] = jnp.zeros((8 - 2 * mates, sticks), F32)
+        for g in range(groups):
+            at = (groups - 1 - g) * mates
+            both = [planes[s][at + b, c : c + 1] for c in range(2) for b in range(mates)]
+            all_zeds[source, : 2 * mates, g * per : (g + 1) * per] = jnp.concatenate(both, axis=0)
+
+    lanes = all_zeds.shape[0] * all_zeds.shape[1]
+    total = dot_nt(back.astype(BF16), all_zeds[...].reshape(lanes, sticks).astype(BF16))
+    back = back.astype(BF16).astype(F32)
     for g in range(groups):
-        out_ref[g, 2:4, : 2 * bands] = total
-        out_ref[g, 2:4, 2 * bands :] = jnp.zeros((2, per - 2 * bands), F32)
-
-
-def tail_kernel(bands, scale, recv_ref, sticks_ref, table_ref, out_ref, corr_ref):
+        out_ref[groups - 1 - g, 0:2] = back[:, g * per : (g + 1) * per]
+        out_ref[groups - 1 - g, 2:4, :lanes] = total
+        out_ref[groups - 1 - g, 2:4, lanes:] = jnp.zeros((2, per - lanes), F32)
+
+
+def tail_kernel(mates, scale, recv_ref, sticks_ref, table_ref, out_ref, corr_ref):
     groups, _, stick_dev = recv_ref.shape
     box_edge = out_ref.shape[2]
     sphere = own_sphere(sticks_ref, stick_dev, box_edge)
-    back = jnp.concatenate([recv_ref[:, 0], recv_ref[:, 1]], axis=0).astype(BF16)
+    rows = [recv_ref[groups - 1 - g, c : c + 1] for c in range(2) for g in range(groups)]
+    back = jnp.concatenate(rows, axis=0).astype(BF16)
     values = dot_tn(back, table_ref[...])
     for c in range(2):
         out_ref[c] = jnp.where(sphere, values[:, c * box_edge : (c + 1) * box_edge], 0.0).astype(BF16)
     total = recv_ref[0, 2:4]
     for g in range(1, groups):
         total = total + recv_ref[g, 2:4]
-    real_row = total[0:1] * scale
-    imag_row = total[1:2] * scale
-    corr_ref[0] = real_row[:, :bands] + imag_row[:, bands : 2 * bands]
-    corr_ref[1] = imag_row[:, :bands] - real_row[:, bands : 2 * bands]
+    total = total * scale
+    for q in range(corr_ref.shape[2] // mates):
+        re, im = slice(8 * q, 8 * q + mates), slice(8 * q + mates, 8 * q + 2 * mates)
+        corr_ref[0, :, q * mates : (q + 1) * mates] = total[0:1, re] + total[1:2, im]
+        corr_ref[1, :, q * mates : (q + 1) * mates] = total[1:2, re] - total[0:1, im]
 
 
 def local(band_coeffs, potential, stick_list):
     groups = lax.axis_size("pw")
-    bands = lax.axis_size("band") * band_coeffs.shape[0]
+    bands = lax.axis_size("band")
     _, _, stick_dev, box_edge = band_coeffs.shape
     grid_len = potential.shape[1]
     slab_len = potential.shape[0] * groups
@@ -201,32 +252,82 @@
     columns = stick_list.T
     fwd, transposed = plane_tables(box_edge, grid_len)
     z_inverse, z_forward = z_tables(box_edge, slab_len, grid_len)
-
-    send = pl.pallas_call(
-        functools.partial(head_kernel, bands),
-        out_shape=jax.ShapeDtypeStruct((bands * groups, 2, stick_dev), F32),
-        compiler_params=pltpu.CompilerParams(vmem_limit_bytes=4 << 20),
+    in_hbm = functools.partial(pltpu.with_memory_space_constraint, memory_space=pltpu.HBM)
+    hbm, vmem = pl.BlockSpec(memory_space=pltpu.HBM), pl.BlockSpec(memory_space=pltpu.VMEM)
+    mates = 2 if bands % 2 == 0 else 1
+    count = bands // mates
+
+    send, *operands = pl.pallas_call(
+        functools.partial(head_kernel, mates),
+        out_shape=[
+            jax.ShapeDtypeStruct((mates * groups, 2, stick_dev), F32),
+            jax.ShapeDtypeStruct((box_edge, sticks), BF16),
+            jax.ShapeDtypeStruct((box_edge, sticks), BF16),
+            jax.ShapeDtypeStruct((grid_len, grid_len), BF16),
+            jax.ShapeDtypeStruct(fwd.shape, BF16),
+            jax.ShapeDtypeStruct(transposed.shape, BF16),
+        ],
+        in_specs=[hbm] * 6,
+        out_specs=[vmem] * 6,
+        scratch_shapes=[
+            pltpu.VMEM((2, stick_dev, box_edge), BF16),
+            pltpu.VMEM((2, sticks), jnp.int32),
+            pltpu.VMEM(z_inverse.shape, BF16),
+            pltpu.SemaphoreType.DMA((6,)),
+        ],
+        compiler_params=pltpu.CompilerParams(vmem_limit_bytes=8 << 20),
         name="head",
-    )(band_coeffs[0], columns, z_inverse)
-    planes = lax.all_to_all(send, ("band", "pw"), split_axis=0, concat_axis=0, tiled=True)
-    backs = pl.pallas_call(
-        functools.partial(plane_kernel, bands),
-        out_shape=jax.ShapeDtypeStruct((groups, 4, stick_dev), F32),
+    )(
+        in_hbm(band_coeffs[0]),
+        in_hbm(columns),
+        in_hbm(z_inverse),
+        in_hbm(potential[0]),
+        in_hbm(fwd),
+        in_hbm(transposed),
+    )
+    hot_a, hot_b = operands[:2]
+    order = [
+        [(q * mates + b) * groups + g for g in reversed(range(groups)) for b in range(mates)] for q in range(count)
+    ]
+    planes = lax.all_to_all(
+        send, ("band", "pw"), split_axis=0, concat_axis=0, tiled=True, axis_index_groups=order
+    )
+    others = [
+        lax.ppermute(planes, "band", [(b, (b + s * mates) % bands) for b in range(bands)]) for s in range(1, count)
+    ]
+    cell = pl.pallas_call(
+        functools.partial(plane_kernel, mates),
+        out_shape=jax.ShapeDtypeStruct((2 * box_edge, box_edge), BF16),
+        in_specs=[vmem] * 6,
+        out_specs=vmem,
         scratch_shapes=[
-            pltpu.VMEM((box_edge, sticks), BF16),
-            pltpu.VMEM((box_edge, sticks), BF16),
             pltpu.VMEM((2 * box_edge, sticks), BF16),
             pltpu.VMEM((2, box_edge, grid_len), BF16),
             pltpu.VMEM((2, grid_len, box_edge), BF16),
-            pltpu.VMEM((2 * box_edge, box_edge), BF16),
-            pltpu.VMEM((2 * bands, sticks), BF16),
         ],
-        compiler_params=pltpu.CompilerParams(vmem_limit_bytes=32 << 20),
+        compiler_params=pltpu.CompilerParams(vmem_limit_bytes=16 << 20),
+        cost_estimate=pl.CostEstimate(flops=1_400_000_000, bytes_accessed=3 << 20, transcendentals=0),
         name="plane",
-    )(planes, potential[0], columns, fwd, transposed)
-    back = lax.all_to_all(backs, "pw", split_axis=0, concat_axis=0, tiled=True)
+    )(planes, *operands)
+    backs = pl.pallas_call(
+        functools.partial(read_kernel, mates, count),
+        out_shape=jax.ShapeDtypeStruct((groups, 4, stick_dev), F32),
+        in_specs=[vmem] * (3 + count),
+        out_specs=vmem,
+        scratch_shapes=[pltpu.VMEM((count, 8, sticks), F32)],
+        compiler_params=pltpu.CompilerParams(vmem_limit_bytes=16 << 20),
+        name="read",
+    )(cell, hot_a, hot_b, planes, *others)
+    back = lax.all_to_all(
+        backs,
+        "pw",
+        split_axis=0,
+        concat_axis=0,
+        tiled=True,
+        axis_index_groups=[list(reversed(range(groups)))],
+    )
     applied, correlation = pl.pallas_call(
-        functools.partial(tail_kernel, bands, 1.0 / math.sqrt(slab_len * sticks)),
+        functools.partial(tail_kernel, mates, 1.0 / math.sqrt(slab_len * sticks)),
         out_shape=[
             jax.ShapeDtypeStruct((2, stick_dev, box_edge), BF16),
             jax.ShapeDtypeStruct((2, 1, bands), F32),

time: 34.2 us -> 27.8 us (0.81)
  local copies, waits for them, and re-layouts: 5.43 us -> 0.01 us
  blocking collectives: 23.4 us -> 20 us
  starting transfers between devices: 0 us -> 1.49 us
  Pallas kernels: 4.24 us -> 5.04 us
    unnamed x16 -> x4, local copies, waits for them, and re-layouts: 5.43 us -> 0.01 us
    all_to_all x1, blocking collectives: 14.3 us -> 10.8 us  [local(): lax.all_to_all(send, ('band', 'pw'), split_axis=0, concat_axis=0, tiled=T...]
    ppermute x0 -> x1, starting transfers between devices: none -> 1.49 us  [local(): lax.ppermute(planes, 'band', [(b, (b + s * mates) % bands) for b in range...]
    pallas_call x3 -> x4, Pallas kernels: 4.24 us -> 5.04 us  [the longest x1 1.99 us: local(): pl.pallas_call(functools.partial(plane_kernel, mates), out_shape=jax.Shap...]
  transfers between devices with their start and end apart: 0 -> 1, of which waited for: 0 -> 1; matrix products, arithmetic and copies ran while one was open for 0% -> 0% of each run, Pallas kernels for 0% -> 7%
where the time goes in v2:
time: 27.8 us; the launch traced here: 27.5 us
  blocking collectives  20 us (72%)
  Pallas kernels  5.04 us (18%)
  starting transfers between devices  1.49 us (5%)
  between operations  0.66 us (2%)
    all_to_all x1, blocking collectives, local(): lax.all_to_all(send, ('band', 'pw'), split_axis=0, concat_axis=0, tiled=T...  10.8 us
    all_to_all x1, blocking collectives, local(): lax.all_to_all(backs, 'pw', split_axis=0, concat_axis=0, tiled=True, axis...  9.21 us
    pallas_call x1, Pallas kernels, local(): pl.pallas_call(functools.partial(plane_kernel, mates), out_shape=jax.Shap...  1.99 us
    pallas_call x1, Pallas kernels, local(): pl.pallas_call(functools.partial(head_kernel, mates), out_shape=[jax.Shap...  1.52 us
    ppermute x1, starting transfers between devices, local(): lax.ppermute(planes, 'band', [(b, (b + s * mates) % bands) for b in range...  1.49 us
    pallas_call x1, Pallas kernels, local(): pl.pallas_call(functools.partial(tail_kernel, mates, 1.0 / math.sqrt(slab...  0.9 us
    pallas_call x1, Pallas kernels, local(): pl.pallas_call(functools.partial(read_kernel, mates, count), out_shape=ja...  0.64 us
  transfers between devices with their start and end apart: 1, of which 1 were waited for; matrix products, arithmetic and copies ran while one was open for 0% of the time, Pallas kernels for 7%

profile of v2, /device:TPU:0, one launch (start us, length us, event | category | flops | bytes accessed | tf_op | source)
XLA Modules:
  0.0 27.5 jit_solution(8940113369790341218)
XLA Ops:
  0.6 1.5 %head.1 = (f32[16,2,128]{2,1,0:T(2,128)S(1)}, bf16[256,1024]{1,0:T(8,128)(2,1)S(1)}, bf16[256,1024]{1,0:T(8,128)(2,1)S(1)}, bf16[512,512]{1,0:T(8,128)(2,1)S(1)}...) custom-call(bf16[2,128,256]{2,1,0:T(8,128)(2,1)} %bitcast.10, s32[2,1024]{1,0:T(2,128)} %bitcast.7, ...), custom_call_target="tpu_custom_call" | custom-call | tf_op jit(solution)/shard_map/head/pallas_call | solution.py:260
  2.2 10.8 %all_to_all.10.recv_ref.refs_3_ = f32[16,2,128]{2,1,0:T(2,128)S(1)} all-to-all(f32[16,2,128]{2,1,0:T(2,128)S(1)} %get-tuple-element.10), channel_id=1, replica_groups={{7,15,6,14,5,13,4,12,3,11,2,10,1,9,0,8},{23,31,22,30,21,29,20,28,19,27,..., dimensions={0} | all-to-all | bytes 32768 | tf_op jit(solution)/shard_map/all_to_all | solution.py:292
  13.0 1.5 %collective-permute-start = (f32[16,2,128]{2,1,0:T(2,128)S(1)}, f32[16,2,128]{2,1,0:T(2,128)S(1)}, u32[]{:S(2)}, u32[]{:S(2)}) collective-permute-start(f32[16,2,128]{2,1,0:T(2,128)S(1)} %all_to_all.10.recv_ref.refs_3_), channel_id=1, source_target_pairs={{0,16},{8,24},{16,0},{24,8},{1,17},{9,25},{17,1},{25,9},{2,18},{10... | collective-permute-start | bytes 49160 | tf_op jit(solution)/shard_map/ppermute | solution.py:296
  14.5 2.0 %plane.1.refs_0_ = bf16[512,256]{1,0:T(8,128)(2,1)S(1)} custom-call(f32[16,2,128]{2,1,0:T(2,128)S(1)} %all_to_all.10.recv_ref.refs_3_, bf16[256,1024]{1,0:T(8,128)(2,1)S(1)} %get-tuple-element.11.hot_a.refs_1_, bf16[256,1024]{1,0:T(8,128)(2,1)S(1)} %get-tuple-element.12.hot_b.refs_2_, bf16[512,512]{1,0:T(8,128)(2,1)S(1)} %get-tuple-element.13.pot_ref, ...), custom_call_target="tpu_custom_call" | custom-call | flops 1400000000 | bytes 3145728 | tf_op jit(solution)/shard_map/plane/pallas_call | solution.py:298
  16.5 0.3 collective-permute-done.refs_4_
  16.7 0.6 %read.1 = f32[8,4,128]{2,1,0:T(4,128)S(1)} custom-call(bf16[512,256]{1,0:T(8,128)(2,1)S(1)} %plane.1.refs_0_, bf16[256,1024]{1,0:T(8,128)(2,1)S(1)} %get-tuple-element.11.hot_a.refs_1_, bf16[256,1024]{1,0:T(8,128)(2,1)S(1)} %get-tuple-element.12.hot_b.refs_2_, f32[16,2,128]{2,1,0:T(2,128)S(1)} %all_to_all.10.recv_ref.refs_3_, ...), custom_call_target="tpu_custom_call" | custom-call | tf_op jit(solution)/shard_map/read/pallas_call | solution.py:312
  17.4 0.0 copy-start
  17.4 0.0 copy-start.1
  17.4 9.2 %all_to_all.11.recv_ref = f32[8,4,128]{2,1,0:T(4,128)S(1)} all-to-all(f32[8,4,128]{2,1,0:T(4,128)S(1)} %read.1), channel_id=1, replica_groups={{7,6,5,4,3,2,1,0},{15,14,13,12,11,10,9,8},{23,22,21,20,19,18,17,16},{31..., dimensions={0} | all-to-all | bytes 32768 | tf_op jit(solution)/shard_map/all_to_all | solution.py:321
  26.6 0.0 copy-done
  26.6 0.0 copy-done.1
  26.6 0.9 %tail.1 = (bf16[2,128,256]{2,1,0:T(8,128)(2,1)}, f32[2,1,4]{2,1,0:T(1,128)}) custom-call(f32[8,4,128]{2,1,0:T(4,128)S(1)} %all_to_all.11.recv_ref, s32[2,1024]{1,0:T(2,128)S(1)} %bitcast.8, bf16[16,512]{1,0:T(8,128)(2,1)S(1)} %copy-done.1), custom_call_target="tpu_custom_call" | custom-call | tf_op jit(solution)/shard_map/tail/pallas_call | solution.py:329
Async XLA Ops:
  13.0 3.7 %collective-permute-start = (f32[16,2,128]{2,1,0:T(2,128)S(1)}, f32[16,2,128]{2,1,0:T(2,128)S(1)}, u32[]{:S(2)}, u32[]{:S(2)}) collective-permute-start(f32[16,2,128]{2,1,0:T(2,128)S(1)} %all_to_all.10.recv_ref.refs_3_), channel_id=1, source_target_pairs={{0,16},{8,24},{16,0},{24,8},{1,17},{9,25},{17,1},{25,9},{2,18},{10... | collective-permute-start | bytes 49160 | tf_op jit(solution)/shard_map/ppermute | solution.py:296
  17.4 9.2 %copy-start = (s32[1024,2]{0,1:T(2,128)S(1)}, s32[1024,2]{0,1:T(2,128)}, u32[]{:S(2)}) copy-start(s32[1024,2]{0,1:T(2,128)} %param.9) | copy-start | bytes 24580
  17.4 9.2 %copy-start.1 = (bf16[16,512]{1,0:T(8,128)(2,1)S(1)}, bf16[16,512]{1,0:T(8,128)(2,1)}, u32[]{:S(2)}) copy-start(bf16[16,512]{1,0:T(8,128)(2,1)} %constant.11.clone.table_ref) | copy-start | bytes 49156

commit v3 on v2

--- a/solution.py
+++ b/solution.py
@@ -11,6 +11,12 @@
 
 F32 = jnp.float32
 BF16 = jnp.bfloat16
+
+
+def led(group, mate, groups, mates):
+    members = [(g, b) for g in range(groups) for b in range(mates)]
+    members.remove((group, mate))
+    return [(group, mate), *members]
 
 
 def phases(box_index, grid_index, period, factor):
@@ -63,6 +69,7 @@
 
 def head_kernel(
     mates,
+    first,
     coeffs_hbm,
     sticks_hbm,
     table_hbm,
@@ -110,7 +117,7 @@
     for z in range(slab_len):
         row = jnp.concatenate([real[z : z + 1], imag[z : z + 1]], axis=0)
         for b in range(mates):
-            out_ref[(slab_len - 1 - z) * mates + b] = row
+            out_ref[first.index((z, b))] = row
 
     codes = sticks_ref[...]
     codes = (codes & 1) * side + (codes >> 1)
@@ -124,7 +131,7 @@
 
 
 def plane_kernel(
-    mates, recv_ref, hot_a, hot_b, pot_ref, fwd_ref, tr_ref, cell_ref, spread, half_ref, mid_ref
+    mates, first, recv_ref, hot_a, hot_b, pot_ref, fwd_ref, tr_ref, cell_ref, spread, half_ref, mid_ref
 ):
     box_edge, sticks = hot_a.shape
     side = box_edge // 2
@@ -136,8 +143,10 @@
     own_mate = lax.rem(lax.axis_index("band"), mates)
     for g in range(groups):
         cols = slice(g * per, (g + 1) * per)
-        at = (groups - 1 - g) * mates
-        own = recv_ref[at + own_mate].astype(BF16)
+        own = recv_ref[first.index((g, 0))]
+        for b in range(1, mates):
+            own = jnp.where(own_mate == b, recv_ref[first.index((g, b))], own)
+        own = own.astype(BF16)
         for c in range(2):
             placed = hot_b[:, cols] * own[c : c + 1]
             for p in range(2):
@@ -182,13 +191,13 @@
         cell_ref[p * box_edge : (p + 1) * box_edge] = cell.astype(BF16)
 
 
-def read_kernel(mates, count, *refs):
+def read_kernel(mates, count, first, second, *refs):
     cell_ref, hot_a, hot_b = refs[:3]
     planes = refs[3 : 3 + count]
     out_ref, all_zeds = refs[3 + count :]
     box_edge, sticks = hot_a.shape
     side = box_edge // 2
-    groups = out_ref.shape[0]
+    groups = out_ref.shape[0] // mates
     per = sticks // groups
 
     backs = [[], []]
@@ -210,31 +219,39 @@
         source = lax.rem(here - s + count, count)
         all_zeds[source, 2 * mates :] = jnp.zeros((8 - 2 * mates, sticks), F32)
         for g in range(groups):
-            at = (groups - 1 - g) * mates
-            both = [planes[s][at + b, c : c + 1] for c in range(2) for b in range(mates)]
+            both = [planes[s][first.index((g, b)), c : c + 1] for c in range(2) for b in range(mates)]
             all_zeds[source, : 2 * mates, g * per : (g + 1) * per] = jnp.concatenate(both, axis=0)
 
     lanes = all_zeds.shape[0] * all_zeds.shape[1]
     total = dot_nt(back.astype(BF16), all_zeds[...].reshape(lanes, sticks).astype(BF16))
     back = back.astype(BF16).astype(F32)
     for g in range(groups):
-        out_ref[groups - 1 - g, 0:2] = back[:, g * per : (g + 1) * per]
-        out_ref[groups - 1 - g, 2:4, :lanes] = total
-        out_ref[groups - 1 - g, 2:4, lanes:] = jnp.zeros((2, per - lanes), F32)
-
-
-def tail_kernel(mates, scale, recv_ref, sticks_ref, table_ref, out_ref, corr_ref):
-    groups, _, stick_dev = recv_ref.shape
+        for b in range(mates):
+            at = second.index((g, b))
+            out_ref[at, 0:2] = back[:, g * per : (g + 1) * per]
+            out_ref[at, 2:4, :lanes] = total
+            out_ref[at, 2:4, lanes:] = jnp.zeros((2, per - lanes), F32)
+
+
+def tail_kernel(mates, second, scale, recv_ref, sticks_ref, table_ref, out_ref, corr_ref):
+    blocks, _, stick_dev = recv_ref.shape
+    groups = blocks // mates
+    own_mate = lax.rem(lax.axis_index("band"), mates)
     box_edge = out_ref.shape[2]
     sphere = own_sphere(sticks_ref, stick_dev, box_edge)
-    rows = [recv_ref[groups - 1 - g, c : c + 1] for c in range(2) for g in range(groups)]
-    back = jnp.concatenate(rows, axis=0).astype(BF16)
+    picked = []
+    for g in range(groups):
+        own = recv_ref[second.index((g, 0))]
+        for b in range(1, mates):
+            own = jnp.where(own_mate == b, recv_ref[second.index((g, b))], own)
+        picked.append(own)
+    back = jnp.concatenate([own[c : c + 1] for c in range(2) for own in picked], axis=0).astype(BF16)
     values = dot_tn(back, table_ref[...])
     for c in range(2):
         out_ref[c] = jnp.where(sphere, values[:, c * box_edge : (c + 1) * box_edge], 0.0).astype(BF16)
-    total = recv_ref[0, 2:4]
-    for g in range(1, groups):
-        total = total + recv_ref[g, 2:4]
+    total = picked[0][2:4]
+    for own in picked[1:]:
+        total = total + own[2:4]
     total = total * scale
     for q in range(corr_ref.shape[2] // mates):
         re, im = slice(8 * q, 8 * q + mates), slice(8 * q + mates, 8 * q + 2 * mates)
@@ -256,9 +273,11 @@
     hbm, vmem = pl.BlockSpec(memory_space=pltpu.HBM), pl.BlockSpec(memory_space=pltpu.VMEM)
     mates = 2 if bands % 2 == 0 else 1
     count = bands // mates
+    first = led(groups - 1, 1, groups, mates)
+    second = led(groups - 1, 1, groups, mates)
 
     send, *operands = pl.pallas_call(
-        functools.partial(head_kernel, mates),
+        functools.partial(head_kernel, mates, first),
         out_shape=[
             jax.ShapeDtypeStruct((mates * groups, 2, stick_dev), F32),
             jax.ShapeDtypeStruct((box_edge, sticks), BF16),
@@ -286,9 +305,7 @@
         in_hbm(transposed),
     )
     hot_a, hot_b = operands[:2]
-    order = [
-        [(q * mates + b) * groups + g for g in reversed(range(groups)) for b in range(mates)] for q in range(count)
-    ]
+    order = [[(q * mates + b) * groups + g for g, b in first] for q in range(count)]
     planes = lax.all_to_all(
         send, ("band", "pw"), split_axis=0, concat_axis=0, tiled=True, axis_index_groups=order
     )
@@ -296,7 +313,7 @@
         lax.ppermute(planes, "band", [(b, (b + s * mates) % bands) for b in range(bands)]) for s in range(1, count)
     ]
     cell = pl.pallas_call(
-        functools.partial(plane_kernel, mates),
+        functools.partial(plane_kernel, mates, first),
         out_shape=jax.ShapeDtypeStruct((2 * box_edge, box_edge), BF16),
         in_specs=[vmem] * 6,
         out_specs=vmem,
@@ -310,8 +327,8 @@
         name="plane",
     )(planes, *operands)
     backs = pl.pallas_call(
-        functools.partial(read_kernel, mates, count),
-        out_shape=jax.ShapeDtypeStruct((groups, 4, stick_dev), F32),
+        functools.partial(read_kernel, mates, count, first, second),
+        out_shape=jax.ShapeDtypeStruct((mates * groups, 4, stick_dev), F32),
         in_specs=[vmem] * (3 + count),
         out_specs=vmem,
         scratch_shapes=[pltpu.VMEM((count, 8, sticks), F32)],
@@ -320,14 +337,14 @@
     )(cell, hot_a, hot_b, planes, *others)
     back = lax.all_to_all(
         backs,
-        "pw",
+        ("band", "pw"),
         split_axis=0,
         concat_axis=0,
         tiled=True,
-        axis_index_groups=[list(reversed(range(groups)))],
+        axis_index_groups=[[(q * mates + b) * groups + g for g, b in second] for q in range(count)],
     )
     applied, correlation = pl.pallas_call(
-        functools.partial(tail_kernel, mates, 1.0 / math.sqrt(slab_len * sticks)),
+        functools.partial(tail_kernel, mates, second, 1.0 / math.sqrt(slab_len * sticks)),
         out_shape=[
             jax.ShapeDtypeStruct((2, stick_dev, box_edge), BF16),
             jax.ShapeDtypeStruct((2, 1, bands), F32),

time: 27.8 us -> 26.5 us (0.953)
  blocking collectives: 20 us -> 18.8 us
    all_to_all x1, blocking collectives: 9.21 us -> 8.41 us  [local(): lax.all_to_all(backs, ('band', 'pw'), split_axis=0, concat_axis=0, tiled=...]
    all_to_all x1, blocking collectives: 10.8 us -> 10.3 us  [local(): lax.all_to_all(send, ('band', 'pw'), split_axis=0, concat_axis=0, tiled=T...]
  transfers between devices with their start and end apart: 1 -> 1, of which waited for: 1 -> 1; matrix products, arithmetic and copies ran while one was open for 0% -> 0% of each run, Pallas kernels for 7% -> 8%
where the time goes in v3:
time: 26.5 us; the launch traced here: 26.3 us
  blocking collectives  18.8 us (71%)
  Pallas kernels  5.07 us (19%)
  starting transfers between devices  1.49 us (6%)
  between operations  0.67 us (3%)
    all_to_all x1, blocking collectives, local(): lax.all_to_all(send, ('band', 'pw'), split_axis=0, concat_axis=0, tiled=T...  10.3 us
    all_to_all x1, blocking collectives, local(): lax.all_to_all(backs, ('band', 'pw'), split_axis=0, concat_axis=0, tiled=...  8.41 us
    pallas_call x1, Pallas kernels, local(): pl.pallas_call(functools.partial(plane_kernel, mates, first), out_shape=j...  1.99 us
    pallas_call x1, Pallas kernels, local(): pl.pallas_call(functools.partial(head_kernel, mates, first), out_shape=[j...  1.52 us
    ppermute x1, starting transfers between devices, local(): lax.ppermute(planes, 'band', [(b, (b + s * mates) % bands) for b in range...  1.49 us
    pallas_call x1, Pallas kernels, local(): pl.pallas_call(functools.partial(tail_kernel, mates, second, 1.0 / math.s...  0.91 us
    pallas_call x1, Pallas kernels, local(): pl.pallas_call(functools.partial(read_kernel, mates, count, first, second...  0.65 us
  transfers between devices with their start and end apart: 1, of which 1 were waited for; matrix products, arithmetic and copies ran while one was open for 0% of the time, Pallas kernels for 8%

profile of v3, /device:TPU:0, one launch (start us, length us, event | category | flops | bytes accessed | tf_op | source)
XLA Modules:
  0.0 26.3 jit_solution(9925410585653779429)
XLA Ops:
  0.6 1.5 %head.1 = (f32[16,2,128]{2,1,0:T(2,128)S(1)}, bf16[256,1024]{1,0:T(8,128)(2,1)S(1)}, bf16[256,1024]{1,0:T(8,128)(2,1)S(1)}, bf16[512,512]{1,0:T(8,128)(2,1)S(1)}...) custom-call(bf16[2,128,256]{2,1,0:T(8,128)(2,1)} %bitcast.10, s32[2,1024]{1,0:T(2,128)} %bitcast.7, ...), custom_call_target="tpu_custom_call" | custom-call | tf_op jit(solution)/shard_map/head/pallas_call | solution.py:279
  2.2 10.3 %all_to_all.10.recv_ref.refs_3_ = f32[16,2,128]{2,1,0:T(2,128)S(1)} all-to-all(f32[16,2,128]{2,1,0:T(2,128)S(1)} %get-tuple-element.10), channel_id=1, replica_groups={{15,0,8,1,9,2,10,3,11,4,12,5,13,6,14,7},{31,16,24,17,25,18,26,19,27,20,..., dimensions={0} | all-to-all | bytes 32768 | tf_op jit(solution)/shard_map/all_to_all | solution.py:309
  12.5 1.5 %collective-permute-start = (f32[16,2,128]{2,1,0:T(2,128)S(1)}, f32[16,2,128]{2,1,0:T(2,128)S(1)}, u32[]{:S(2)}, u32[]{:S(2)}) collective-permute-start(f32[16,2,128]{2,1,0:T(2,128)S(1)} %all_to_all.10.recv_ref.refs_3_), channel_id=1, source_target_pairs={{0,16},{8,24},{16,0},{24,8},{1,17},{9,25},{17,1},{25,9},{2,18},{10... | collective-permute-start | bytes 49160 | tf_op jit(solution)/shard_map/ppermute | solution.py:313
  14.0 2.0 %plane.1.refs_0_ = bf16[512,256]{1,0:T(8,128)(2,1)S(1)} custom-call(f32[16,2,128]{2,1,0:T(2,128)S(1)} %all_to_all.10.recv_ref.refs_3_, bf16[256,1024]{1,0:T(8,128)(2,1)S(1)} %get-tuple-element.11.hot_a.refs_1_, bf16[256,1024]{1,0:T(8,128)(2,1)S(1)} %get-tuple-element.12.hot_b.refs_2_, bf16[512,512]{1,0:T(8,128)(2,1)S(1)} %get-tuple-element.13.pot_ref, ...), custom_call_target="tpu_custom_call" | custom-call | flops 1400000000 | bytes 3145728 | tf_op jit(solution)/shard_map/plane/pallas_call | solution.py:315
  16.0 0.2 collective-permute-done.refs_4_
  16.2 0.7 %read.1 = f32[16,4,128]{2,1,0:T(4,128)S(1)} custom-call(bf16[512,256]{1,0:T(8,128)(2,1)S(1)} %plane.1.refs_0_, bf16[256,1024]{1,0:T(8,128)(2,1)S(1)} %get-tuple-element.11.hot_a.refs_1_, bf16[256,1024]{1,0:T(8,128)(2,1)S(1)} %get-tuple-element.12.hot_b.refs_2_, f32[16,2,128]{2,1,0:T(2,128)S(1)} %all_to_all.10.recv_ref.refs_3_, ...), custom_call_target="tpu_custom_call" | custom-call | tf_op jit(solution)/shard_map/read/pallas_call | solution.py:329
  16.9 0.0 copy-start
  16.9 0.0 copy-start.1
  16.9 8.4 %all_to_all.11.recv_ref = f32[16,4,128]{2,1,0:T(4,128)S(1)} all-to-all(f32[16,4,128]{2,1,0:T(4,128)S(1)} %read.1), channel_id=1, replica_groups={{15,0,8,1,9,2,10,3,11,4,12,5,13,6,14,7},{31,16,24,17,25,18,26,19,27,20,..., dimensions={0} | all-to-all | bytes 65536 | tf_op jit(solution)/shard_map/all_to_all | solution.py:338
  25.3 0.0 copy-done
  25.3 0.0 copy-done.1
  25.3 0.9 %tail.1 = (bf16[2,128,256]{2,1,0:T(8,128)(2,1)}, f32[2,1,4]{2,1,0:T(1,128)}) custom-call(f32[16,4,128]{2,1,0:T(4,128)S(1)} %all_to_all.11.recv_ref, s32[2,1024]{1,0:T(2,128)S(1)} %bitcast.8, bf16[16,512]{1,0:T(8,128)(2,1)S(1)} %copy-done.1), custom_call_target="tpu_custom_call" | custom-call | tf_op jit(solution)/shard_map/tail/pallas_call | solution.py:346
Async XLA Ops:
  12.5 3.7 %collective-permute-start = (f32[16,2,128]{2,1,0:T(2,128)S(1)}, f32[16,2,128]{2,1,0:T(2,128)S(1)}, u32[]{:S(2)}, u32[]{:S(2)}) collective-permute-start(f32[16,2,128]{2,1,0:T(2,128)S(1)} %all_to_all.10.recv_ref.refs_3_), channel_id=1, source_target_pairs={{0,16},{8,24},{16,0},{24,8},{1,17},{9,25},{17,1},{25,9},{2,18},{10... | collective-permute-start | bytes 49160 | tf_op jit(solution)/shard_map/ppermute | solution.py:313
  16.9 8.4 %copy-start = (s32[1024,2]{0,1:T(2,128)S(1)}, s32[1024,2]{0,1:T(2,128)}, u32[]{:S(2)}) copy-start(s32[1024,2]{0,1:T(2,128)} %param.9) | copy-start | bytes 24580
  16.9 8.4 %copy-start.1 = (bf16[16,512]{1,0:T(8,128)(2,1)S(1)}, bf16[16,512]{1,0:T(8,128)(2,1)}, u32[]{:S(2)}) copy-start(bf16[16,512]{1,0:T(8,128)(2,1)} %constant.11.clone.table_ref) | copy-start | bytes 49156

commit v4 on v2

--- a/solution.py
+++ b/solution.py
@@ -11,6 +11,10 @@
 
 F32 = jnp.float32
 BF16 = jnp.bfloat16
+
+
+def place_of(group, mate, groups, mates):
+    return (groups - 1 - group) * mates + mates - 1 - mate
 
 
 def phases(box_index, grid_index, period, factor):
@@ -28,12 +32,13 @@
         )
         mats.append(np.block([[cos, sin], [-sin, cos]]))
     mats = np.stack(mats)
-    return jnp.asarray(mats, BF16), jnp.asarray(mats.transpose(0, 2, 1), BF16)
+    return jnp.asarray(mats[:, : box_edge // 2], BF16), jnp.asarray(mats.transpose(0, 2, 1)[:, :half], BF16)
 
 
 def z_tables(box_edge, slab_len, grid_len):
     cos, sin = phases(np.arange(box_edge) - box_edge // 2, np.arange(slab_len), grid_len, 1.0)
-    inverse = np.concatenate([cos.T, sin.T]) / math.sqrt(box_edge)
+    inverse = np.stack([np.concatenate([cos.T, -sin.T], 1), np.concatenate([sin.T, cos.T], 1)], 1)
+    inverse = inverse.reshape(2 * slab_len, 2 * box_edge) / math.sqrt(box_edge)
     forward = np.block([[cos.T, -sin.T], [sin.T, cos.T]]) / math.sqrt(slab_len)
     return jnp.asarray(inverse, BF16), jnp.asarray(forward, BF16)
 
@@ -80,12 +85,13 @@
     table_ref,
     sems,
 ):
+    side, n_half = fwd_hbm.shape[1], tr_hbm.shape[1]
     pairs = [
         (sticks_hbm, sticks_ref),
         (coeffs_hbm, coeffs_ref),
         (table_hbm, table_ref),
-        (fwd_hbm, fwd_ref),
-        (tr_hbm, tr_ref),
+        (fwd_hbm, fwd_ref.at[:, :side]),
+        (tr_hbm, tr_ref.at[:, :n_half]),
         (pot_hbm, pot_ref),
     ]
     copies = [pltpu.make_async_copy(src, dst, sems.at[n]) for n, (src, dst) in enumerate(pairs)]
@@ -93,38 +99,50 @@
         copy.start()
     _, stick_dev, box_edge = coeffs_ref.shape
     slab_len = table_ref.shape[0] // 2
-    side = box_edge // 2
     copies[0].wait()
     sphere = own_sphere(sticks_ref, stick_dev, box_edge)
     copies[1].wait()
     copies[2].wait()
-    table = table_ref[...]
-    parts = []
-    for c in range(2):
-        masked = jnp.where(sphere, coeffs_ref[c].astype(F32), 0.0).astype(BF16)
-        parts.append(dot_nt(table, masked))
-    real = parts[0][:slab_len] - parts[1][slab_len:]
-    imag = parts[0][slab_len:] + parts[1][:slab_len]
-    real = real.astype(BF16).astype(F32)
-    imag = imag.astype(BF16).astype(F32)
+    masked = [jnp.where(sphere, coeffs_ref[c].astype(F32), 0.0).astype(BF16) for c in range(2)]
+    masked = jnp.concatenate(masked, axis=1)
+    rows = dot_nt(table_ref[...], masked).astype(BF16).astype(F32)
     for z in range(slab_len):
-        row = jnp.concatenate([real[z : z + 1], imag[z : z + 1]], axis=0)
         for b in range(mates):
-            out_ref[(slab_len - 1 - z) * mates + b] = row
+            out_ref[place_of(z, b, slab_len, mates)] = rows[2 * z : 2 * z + 2]
 
     codes = sticks_ref[...]
-    codes = (codes & 1) * side + (codes >> 1)
-    rows = lax.broadcasted_iota(jnp.int32, (box_edge, stick_dev), 0)
+    codes = ((codes & 1) * side + (codes >> 1)).astype(F32).astype(BF16)
+    rows = lax.broadcasted_iota(jnp.int32, (box_edge, stick_dev), 0).astype(F32).astype(BF16)
+    one, none = jnp.ones((), BF16), jnp.zeros((), BF16)
     for at in range(0, codes.shape[1], stick_dev):
         cols = slice(at, at + stick_dev)
-        hot_a[:, cols] = jnp.where(rows == codes[0:1, cols], 1.0, 0.0).astype(BF16)
-        hot_b[:, cols] = jnp.where(rows == codes[1:2, cols], 1.0, 0.0).astype(BF16)
-    for copy in copies[3:]:
+        hot_a[:, cols] = jnp.where(rows == codes[0:1, cols], one, none)
+        hot_b[:, cols] = jnp.where(rows == codes[1:2, cols], one, none)
+    for copy in copies[3:5]:
         copy.wait()
+    for p in range(2):
+        fwd_ref[p, side:, :n_half] = -fwd_ref[p, :side, n_half:]
+        fwd_ref[p, side:, n_half:] = fwd_ref[p, :side, :n_half]
+        tr_ref[p, n_half:, :side] = -tr_ref[p, :n_half, side:]
+        tr_ref[p, n_half:, side:] = tr_ref[p, :n_half, :side]
+    copies[5].wait()
 
 
 def plane_kernel(
-    mates, recv_ref, hot_a, hot_b, pot_ref, fwd_ref, tr_ref, cell_ref, spread, half_ref, mid_ref
+    mates,
+    recv_ref,
+    hot_a,
+    hot_b,
+    pot_ref,
+    fwd_ref,
+    tr_ref,
+    out_ref,
+    back_ref,
+    zeds_ref,
+    spread,
+    half_ref,
+    mid_ref,
+    cell_ref,
 ):
     box_edge, sticks = hot_a.shape
     side = box_edge // 2
@@ -136,8 +154,7 @@
     own_mate = lax.rem(lax.axis_index("band"), mates)
     for g in range(groups):
         cols = slice(g * per, (g + 1) * per)
-        at = (groups - 1 - g) * mates
-        own = recv_ref[at + own_mate].astype(BF16)
+        own = recv_ref[place_of(g, own_mate, groups, mates)].astype(BF16)
         for c in range(2):
             placed = hot_b[:, cols] * own[c : c + 1]
             for p in range(2):
@@ -156,7 +173,7 @@
             half_ref[p, c * side : (c + 1) * side, :n_half] = low[rows, cols]
             half_ref[p, c * side : (c + 1) * side, n_half:] = high[rows, cols]
 
-    step = 128
+    step = 256
     for x0 in range(0, n_half, step):
         sums = {}
         for c in range(2):
@@ -182,64 +199,77 @@
         cell_ref[p * box_edge : (p + 1) * box_edge] = cell.astype(BF16)
 
 
-def read_kernel(mates, count, *refs):
-    cell_ref, hot_a, hot_b = refs[:3]
-    planes = refs[3 : 3 + count]
-    out_ref, all_zeds = refs[3 + count :]
-    box_edge, sticks = hot_a.shape
-    side = box_edge // 2
-    groups = out_ref.shape[0]
-    per = sticks // groups
-
-    backs = [[], []]
     wide = 256
     for s0 in range(0, sticks, wide):
         cols = slice(s0, s0 + wide)
         picked = dot_nn(cell_ref[...], hot_b[:, cols])
+        parts = []
         for c in range(2):
             value = None
             for p in range(2):
                 at = p * box_edge + c * side
                 term = picked[at : at + side] * hot_a[p * side : (p + 1) * side, cols].astype(F32)
                 value = term if value is None else value + term
-            backs[c].append(jnp.sum(value, axis=0, keepdims=True))
-    back = jnp.concatenate([jnp.concatenate(parts, axis=1) for parts in backs], axis=0)
-
+            parts.append(jnp.sum(value, axis=0, keepdims=True))
+        back = jnp.concatenate(parts, axis=0).astype(BF16).astype(F32)
+        back_ref[:, cols] = back
+        for g in range(s0 // per, (s0 + wide) // per):
+            for b in range(mates):
+                out_ref[place_of(g, b, groups, mates), 0:2] = back[:, g * per - s0 : (g + 1) * per - s0]
+    gather_rows(mates, recv_ref, zeds_ref)
+
+
+def gather_rows(mates, recv_ref, rows_ref):
+    groups, per = recv_ref.shape[0] // mates, recv_ref.shape[2]
+    for g in range(groups):
+        for b in range(mates):
+            rows_ref[2 * b : 2 * b + 2, g * per : (g + 1) * per] = recv_ref[place_of(g, b, groups, mates)]
+    rows_ref[2 * mates :] = jnp.zeros((8 - 2 * mates, rows_ref.shape[1]), F32)
+
+
+def pair_kernel(mates, count, blocks_ref, back_ref, zeds_ref, *refs):
+    others, out_ref, all_zeds = refs[: count - 1], refs[count - 1], refs[count]
+    del blocks_ref
+    sticks = back_ref.shape[1]
     here = lax.axis_index("band") // mates
-    for s in range(count):
-        source = lax.rem(here - s + count, count)
-        all_zeds[source, 2 * mates :] = jnp.zeros((8 - 2 * mates, sticks), F32)
-        for g in range(groups):
-            at = (groups - 1 - g) * mates
-            both = [planes[s][at + b, c : c + 1] for c in range(2) for b in range(mates)]
-            all_zeds[source, : 2 * mates, g * per : (g + 1) * per] = jnp.concatenate(both, axis=0)
-
-    lanes = all_zeds.shape[0] * all_zeds.shape[1]
-    total = dot_nt(back.astype(BF16), all_zeds[...].reshape(lanes, sticks).astype(BF16))
-    back = back.astype(BF16).astype(F32)
-    for g in range(groups):
-        out_ref[groups - 1 - g, 0:2] = back[:, g * per : (g + 1) * per]
-        out_ref[groups - 1 - g, 2:4, :lanes] = total
-        out_ref[groups - 1 - g, 2:4, lanes:] = jnp.zeros((2, per - lanes), F32)
-
-
-def tail_kernel(mates, scale, recv_ref, sticks_ref, table_ref, out_ref, corr_ref):
-    groups, _, stick_dev = recv_ref.shape
+    all_zeds[here] = zeds_ref[...]
+    for s in range(1, count):
+        gather_rows(mates, others[s - 1], all_zeds.at[lax.rem(here - s + count, count)])
+    lanes = 8 * count
+    total = dot_nt(back_ref[...].astype(BF16), all_zeds[...].reshape(lanes, sticks).astype(BF16))
+    for block in range(out_ref.shape[0]):
+        out_ref[block, 2:4, :lanes] = total
+        out_ref[block, 2:4, lanes:] = jnp.zeros((2, out_ref.shape[2] - lanes), F32)
+
+
+def tail_kernel(mates, scale, recv_ref, sticks_ref, table_ref, out_hbm, corr_hbm, out_ref, corr_ref, sems):
+    blocks, _, stick_dev = recv_ref.shape
+    groups = blocks // mates
+    own_mate = lax.rem(lax.axis_index("band"), mates)
     box_edge = out_ref.shape[2]
-    sphere = own_sphere(sticks_ref, stick_dev, box_edge)
-    rows = [recv_ref[groups - 1 - g, c : c + 1] for c in range(2) for g in range(groups)]
-    back = jnp.concatenate(rows, axis=0).astype(BF16)
-    values = dot_tn(back, table_ref[...])
-    for c in range(2):
-        out_ref[c] = jnp.where(sphere, values[:, c * box_edge : (c + 1) * box_edge], 0.0).astype(BF16)
-    total = recv_ref[0, 2:4]
-    for g in range(1, groups):
-        total = total + recv_ref[g, 2:4]
+    own = [recv_ref[place_of(g, own_mate, groups, mates)] for g in range(groups)]
+    total = own[0][2:4]
+    for part in own[1:]:
+        total = total + part[2:4]
     total = total * scale
     for q in range(corr_ref.shape[2] // mates):
-        re, im = slice(8 * q, 8 * q + mates), slice(8 * q + mates, 8 * q + 2 * mates)
-        corr_ref[0, :, q * mates : (q + 1) * mates] = total[0:1, re] + total[1:2, im]
-        corr_ref[1, :, q * mates : (q + 1) * mates] = total[1:2, re] - total[0:1, im]
+        for b in range(mates):
+            re, im, at = 8 * q + 2 * b, 8 * q + 2 * b + 1, q * mates + b
+            corr_ref[0, :, at : at + 1] = total[0:1, re : re + 1] + total[1:2, im : im + 1]
+            corr_ref[1, :, at : at + 1] = total[1:2, re : re + 1] - total[0:1, im : im + 1]
+    corr_copy = pltpu.make_async_copy(corr_ref, corr_hbm, sems.at[2])
+    corr_copy.start()
+    sphere = own_sphere(sticks_ref, stick_dev, box_edge)
+    back = jnp.concatenate([part[c : c + 1] for c in range(2) for part in own], axis=0).astype(BF16)
+    copies = []
+    for c in range(2):
+        values = dot_tn(back, table_ref[:, c * box_edge : (c + 1) * box_edge])
+        out_ref[c] = jnp.where(sphere, values, 0.0).astype(BF16)
+        copies.append(pltpu.make_async_copy(out_ref.at[c], out_hbm.at[c], sems.at[c]))
+        copies[-1].start()
+    for copy in copies:
+        copy.wait()
+    corr_copy.wait()
 
 
 def local(band_coeffs, potential, stick_list):
@@ -264,8 +294,8 @@
             jax.ShapeDtypeStruct((box_edge, sticks), BF16),
             jax.ShapeDtypeStruct((box_edge, sticks), BF16),
             jax.ShapeDtypeStruct((grid_len, grid_len), BF16),
-            jax.ShapeDtypeStruct(fwd.shape, BF16),
-            jax.ShapeDtypeStruct(transposed.shape, BF16),
+            jax.ShapeDtypeStruct((2, box_edge, grid_len), BF16),
+            jax.ShapeDtypeStruct((2, grid_len, box_edge), BF16),
         ],
         in_specs=[hbm] * 6,
         out_specs=[vmem] * 6,
@@ -285,9 +315,9 @@
         in_hbm(fwd),
         in_hbm(transposed),
     )
-    hot_a, hot_b = operands[:2]
     order = [
-        [(q * mates + b) * groups + g for g in reversed(range(groups)) for b in range(mates)] for q in range(count)
+        [(q * mates + b) * groups + g for g in reversed(range(groups)) for b in reversed(range(mates))]
+        for q in range(count)
     ]
     planes = lax.all_to_all(
         send, ("band", "pw"), split_axis=0, concat_axis=0, tiled=True, axis_index_groups=order
@@ -295,42 +325,56 @@
     others = [
         lax.ppermute(planes, "band", [(b, (b + s * mates) % bands) for b in range(bands)]) for s in range(1, count)
     ]
-    cell = pl.pallas_call(
+    blocks = jax.ShapeDtypeStruct((mates * groups, 4, stick_dev), F32)
+    backs, rows, zeds = pl.pallas_call(
         functools.partial(plane_kernel, mates),
-        out_shape=jax.ShapeDtypeStruct((2 * box_edge, box_edge), BF16),
+        out_shape=[
+            blocks,
+            jax.ShapeDtypeStruct((2, sticks), F32),
+            jax.ShapeDtypeStruct((8, sticks), F32),
+        ],
         in_specs=[vmem] * 6,
-        out_specs=vmem,
+        out_specs=[vmem] * 3,
         scratch_shapes=[
             pltpu.VMEM((2 * box_edge, sticks), BF16),
             pltpu.VMEM((2, box_edge, grid_len), BF16),
             pltpu.VMEM((2, grid_len, box_edge), BF16),
+            pltpu.VMEM((2 * box_edge, box_edge), BF16),
         ],
         compiler_params=pltpu.CompilerParams(vmem_limit_bytes=16 << 20),
         cost_estimate=pl.CostEstimate(flops=1_400_000_000, bytes_accessed=3 << 20, transcendentals=0),
         name="plane",
     )(planes, *operands)
     backs = pl.pallas_call(
-        functools.partial(read_kernel, mates, count),
-        out_shape=jax.ShapeDtypeStruct((groups, 4, stick_dev), F32),
-        in_specs=[vmem] * (3 + count),
+        functools.partial(pair_kernel, mates, count),
+        out_shape=blocks,
+        in_specs=[vmem] * (2 + count),
         out_specs=vmem,
         scratch_shapes=[pltpu.VMEM((count, 8, sticks), F32)],
-        compiler_params=pltpu.CompilerParams(vmem_limit_bytes=16 << 20),
-        name="read",
-    )(cell, hot_a, hot_b, planes, *others)
+        input_output_aliases={0: 0},
+        compiler_params=pltpu.CompilerParams(vmem_limit_bytes=4 << 20),
+        name="pairs",
+    )(backs, rows, zeds, *others)
     back = lax.all_to_all(
         backs,
-        "pw",
+        ("band", "pw"),
         split_axis=0,
         concat_axis=0,
         tiled=True,
-        axis_index_groups=[list(reversed(range(groups)))],
+        axis_index_groups=order,
     )
     applied, correlation = pl.pallas_call(
         functools.partial(tail_kernel, mates, 1.0 / math.sqrt(slab_len * sticks)),
         out_shape=[
             jax.ShapeDtypeStruct((2, stick_dev, box_edge), BF16),
             jax.ShapeDtypeStruct((2, 1, bands), F32),
+        ],
+        in_specs=[vmem] * 3,
+        out_specs=[hbm] * 2,
+        scratch_shapes=[
+            pltpu.VMEM((2, stick_dev, box_edge), BF16),
+            pltpu.VMEM((2, 1, bands), F32),
+            pltpu.SemaphoreType.DMA((3,)),
         ],
         compiler_params=pltpu.CompilerParams(vmem_limit_bytes=4 << 20),
         name="tail",

time: 27.8 us -> 26 us (0.935)
  blocking collectives: 20 us -> 18.8 us
  Pallas kernels: 5.04 us -> 4.7 us
    all_to_all x1, blocking collectives: 9.21 us -> 8.48 us  [local(): lax.all_to_all(backs, ('band', 'pw'), split_axis=0, concat_axis=0, tiled=...]
    all_to_all x1, blocking collectives: 10.8 us -> 10.3 us  [local(): lax.all_to_all(send, ('band', 'pw'), split_axis=0, concat_axis=0, tiled=T...]
  transfers between devices with their start and end apart: 1 -> 1, of which waited for: 1 -> 0; matrix products, arithmetic and copies ran while one was open for 0% -> 0% of each run, Pallas kernels for 7% -> 9%
where the time goes in v4:
time: 26 us; the launch traced here: 25.7 us
  blocking collectives  18.8 us (72%)
  Pallas kernels  4.7 us (18%)
  starting transfers between devices  1.49 us (6%)
  between operations  0.68 us (3%)
    all_to_all x1, blocking collectives, local(): lax.all_to_all(send, ('band', 'pw'), split_axis=0, concat_axis=0, tiled=T...  10.3 us
    all_to_all x1, blocking collectives, local(): lax.all_to_all(backs, ('band', 'pw'), split_axis=0, concat_axis=0, tiled=...  8.48 us
    pallas_call x1, Pallas kernels, local(): pl.pallas_call(functools.partial(plane_kernel, mates), out_shape=[blocks,...  2.26 us
    ppermute x1, starting transfers between devices, local(): lax.ppermute(planes, 'band', [(b, (b + s * mates) % bands) for b in range...  1.49 us
    pallas_call x1, Pallas kernels, local(): pl.pallas_call(functools.partial(head_kernel, mates), out_shape=[jax.Shap...  1.36 us
    pallas_call x1, Pallas kernels, local(): pl.pallas_call(functools.partial(tail_kernel, mates, 1.0 / math.sqrt(slab...  0.92 us
  transfers between devices with their start and end apart: 1, of which 0 were waited for; matrix products, arithmetic and copies ran while one was open for 0% of the time, Pallas kernels for 9%

profile of v4, /device:TPU:0, one launch (start us, length us, event | category | flops | bytes accessed | tf_op | source)
XLA Modules:
  0.0 25.7 jit_solution(9117244393466729783)
XLA Ops:
  0.6 1.4 %head.1 = (f32[16,2,128]{2,1,0:T(2,128)S(1)}, bf16[256,1024]{1,0:T(8,128)(2,1)S(1)}, bf16[256,1024]{1,0:T(8,128)(2,1)S(1)}, bf16[512,512]{1,0:T(8,128)(2,1)S(1)}...) custom-call(bf16[2,128,256]{2,1,0:T(8,128)(2,1)} %bitcast.10, s32[2,1024]{1,0:T(2,128)} %bitcast.7, ...), custom_call_target="tpu_custom_call" | custom-call | tf_op jit(solution)/shard_map/head/pallas_call | solution.py:290
  2.0 10.3 %all_to_all.10.recv_ref = f32[16,2,128]{2,1,0:T(2,128)S(1)} all-to-all(f32[16,2,128]{2,1,0:T(2,128)S(1)} %get-tuple-element.13), channel_id=1, replica_groups={{15,7,14,6,13,5,12,4,11,3,10,2,9,1,8,0},{31,23,30,22,29,21,28,20,27,19,..., dimensions={0} | all-to-all | bytes 32768 | tf_op jit(solution)/shard_map/all_to_all | solution.py:322
  12.3 1.5 %collective-permute-start = (f32[16,2,128]{2,1,0:T(2,128)S(1)}, f32[16,2,128]{2,1,0:T(2,128)S(1)}, u32[]{:S(2)}, u32[]{:S(2)}) collective-permute-start(f32[16,2,128]{2,1,0:T(2,128)S(1)} %all_to_all.10.recv_ref), channel_id=1, source_target_pairs={{0,16},{8,24},{16,0},{24,8},{1,17},{9,25},{17,1},{25,9},{2,18},{10... | collective-permute-start | bytes 49160 | tf_op jit(solution)/shard_map/ppermute | solution.py:326
  13.8 2.3 %plane.1 = (f32[16,4,128]{2,1,0:T(4,128)S(1)}, f32[2,1024]{1,0:T(2,128)S(1)}, f32[8,1024]{1,0:T(8,128)S(1)}) custom-call(f32[16,2,128]{2,1,0:T(2,128)S(1)} %all_to_all.10.recv_ref, bf16[256,1024]{1,0:T(8,128)(2,1)S(1)} %get-tuple-element.14.hot_a, bf16[256,1024]{1,0:T(8,128)(2,1)S(1)} %get-tuple-element.15.hot_b, ...), custom_call_target="tpu_custom_call" | custom-call | flops 1400000000 | bytes 3145728 | tf_op jit(solution)/shard_map/plane/pallas_call | solution.py:329
  16.1 0.0 collective-permute-done.refs_0_
  16.1 0.2 pairs.1
  16.2 0.0 copy-start
  16.3 0.0 copy-start.1
  16.3 8.5 %all_to_all.11.recv_ref = f32[16,4,128]{2,1,0:T(4,128)S(1)} all-to-all(f32[16,4,128]{2,1,0:T(4,128)S(1)} %pairs.1), channel_id=1, replica_groups={{15,7,14,6,13,5,12,4,11,3,10,2,9,1,8,0},{31,23,30,22,29,21,28,20,27,19,..., dimensions={0} | all-to-all | bytes 65536 | tf_op jit(solution)/shard_map/all_to_all | solution.py:358
  24.8 0.0 copy-done
  24.8 0.0 copy-done.1
  24.8 0.9 %tail.1 = (bf16[2,128,256]{2,1,0:T(8,128)(2,1)}, f32[2,1,4]{2,1,0:T(1,128)}) custom-call(f32[16,4,128]{2,1,0:T(4,128)S(1)} %all_to_all.11.recv_ref, s32[2,1024]{1,0:T(2,128)S(1)} %bitcast.8, bf16[16,512]{1,0:T(8,128)(2,1)S(1)} %copy-done.1), custom_call_target="tpu_custom_call" | custom-call | tf_op jit(solution)/shard_map/tail/pallas_call | solution.py:366
Async XLA Ops:
  12.3 3.8 %collective-permute-start = (f32[16,2,128]{2,1,0:T(2,128)S(1)}, f32[16,2,128]{2,1,0:T(2,128)S(1)}, u32[]{:S(2)}, u32[]{:S(2)}) collective-permute-start(f32[16,2,128]{2,1,0:T(2,128)S(1)} %all_to_all.10.recv_ref), channel_id=1, source_target_pairs={{0,16},{8,24},{16,0},{24,8},{1,17},{9,25},{17,1},{25,9},{2,18},{10... | collective-permute-start | bytes 49160 | tf_op jit(solution)/shard_map/ppermute | solution.py:326
  16.2 8.5 %copy-start = (s32[1024,2]{0,1:T(2,128)S(1)}, s32[1024,2]{0,1:T(2,128)}, u32[]{:S(2)}) copy-start(s32[1024,2]{0,1:T(2,128)} %param.9) | copy-start | bytes 24580
  16.3 8.5 %copy-start.1 = (bf16[16,512]{1,0:T(8,128)(2,1)S(1)}, bf16[16,512]{1,0:T(8,128)(2,1)}, u32[]{:S(2)}) copy-start(bf16[16,512]{1,0:T(8,128)(2,1)} %constant.11.clone.table_ref) | copy-start | bytes 49156

commit v5 on v4

--- a/solution.py
+++ b/solution.py
@@ -13,8 +13,21 @@
 BF16 = jnp.bfloat16
 
 
+def first_place(group, groups):
+    return ((groups - 3) - group) % groups
+
+
 def place_of(group, mate, groups, mates):
-    return (groups - 1 - group) * mates + mates - 1 - mate
+    return (groups - 1 - group) % groups * mates + mates - 1 - mate
+
+
+def side_of(mates):
+    band = lax.axis_index("band")
+    return lax.rem(lax.rem(band, mates) + (mates - 1) * (band // mates), mates)
+
+
+def lead_pair(side, mates):
+    return side % mates
 
 
 def phases(box_index, grid_index, period, factor):
@@ -67,7 +80,7 @@
 
 
 def head_kernel(
-    mates,
+    count,
     coeffs_hbm,
     sticks_hbm,
     table_hbm,
@@ -107,8 +120,8 @@
     masked = jnp.concatenate(masked, axis=1)
     rows = dot_nt(table_ref[...], masked).astype(BF16).astype(F32)
     for z in range(slab_len):
-        for b in range(mates):
-            out_ref[place_of(z, b, slab_len, mates)] = rows[2 * z : 2 * z + 2]
+        for t in range(count):
+            out_ref[first_place(z, slab_len) * count + t] = rows[2 * z : 2 * z + 2]
 
     codes = sticks_ref[...]
     codes = ((codes & 1) * side + (codes >> 1)).astype(F32).astype(BF16)
@@ -130,6 +143,7 @@
 
 def plane_kernel(
     mates,
+    count,
     recv_ref,
     hot_a,
     hot_b,
@@ -146,15 +160,15 @@
 ):
     box_edge, sticks = hot_a.shape
     side = box_edge // 2
-    groups = recv_ref.shape[0] // mates
+    groups = recv_ref.shape[0] // count
     per = sticks // groups
     grid_len = pot_ref.shape[0]
     n_half = grid_len // 2
 
-    own_mate = lax.rem(lax.axis_index("band"), mates)
+    own_place = lax.rem(lax.axis_index("band") // mates - lead_pair(side_of(mates), mates) + count, count)
     for g in range(groups):
         cols = slice(g * per, (g + 1) * per)
-        own = recv_ref[place_of(g, own_mate, groups, mates)].astype(BF16)
+        own = recv_ref[first_place(g, groups) * count + own_place].astype(BF16)
         for c in range(2):
             placed = hot_b[:, cols] * own[c : c + 1]
             for p in range(2):
@@ -216,30 +230,35 @@
         for g in range(s0 // per, (s0 + wide) // per):
             for b in range(mates):
                 out_ref[place_of(g, b, groups, mates), 0:2] = back[:, g * per - s0 : (g + 1) * per - s0]
-    gather_rows(mates, recv_ref, zeds_ref)
-
-
-def gather_rows(mates, recv_ref, rows_ref):
-    groups, per = recv_ref.shape[0] // mates, recv_ref.shape[2]
-    for g in range(groups):
-        for b in range(mates):
-            rows_ref[2 * b : 2 * b + 2, g * per : (g + 1) * per] = recv_ref[place_of(g, b, groups, mates)]
-    rows_ref[2 * mates :] = jnp.zeros((8 - 2 * mates, rows_ref.shape[1]), F32)
-
-
-def pair_kernel(mates, count, blocks_ref, back_ref, zeds_ref, *refs):
-    others, out_ref, all_zeds = refs[: count - 1], refs[count - 1], refs[count]
-    del blocks_ref
-    sticks = back_ref.shape[1]
-    here = lax.axis_index("band") // mates
-    all_zeds[here] = zeds_ref[...]
-    for s in range(1, count):
-        gather_rows(mates, others[s - 1], all_zeds.at[lax.rem(here - s + count, count)])
-    lanes = 8 * count
-    total = dot_nt(back_ref[...].astype(BF16), all_zeds[...].reshape(lanes, sticks).astype(BF16))
+    zeds_ref[...] = jnp.zeros_like(zeds_ref)
+    gather_rows(count, 0, recv_ref, zeds_ref)
+
+
+def gather_rows(count, shift, recv_ref, rows_ref):
+    groups, per = recv_ref.shape[0] // count, recv_ref.shape[2]
+    for t in range(count):
+        row = shift * count + t
+        for g in range(groups):
+            block = recv_ref[first_place(g, groups) * count + t]
+            for c in range(2):
+                at = (c * groups + g) * per
+                rows_ref[row : row + 1, at : at + per] = block[c : c + 1]
+
+
+def pair_kernel(mates, count, blocks_ref, seen_ref, back_ref, *refs):
+    others, out_ref, zeds_ref = refs[: mates - 1], refs[mates - 1], refs[mates]
+    del blocks_ref, seen_ref
+    for s in range(1, mates):
+        gather_rows(count, s, others[s - 1], zeds_ref)
+    back = back_ref[...].astype(BF16)
+    left = jnp.concatenate(
+        [jnp.concatenate([back[0:1], back[1:2]], axis=1), jnp.concatenate([back[1:2], -back[0:1]], axis=1)], axis=0
+    )
+    total = dot_nt(left, zeds_ref[...].astype(BF16))
+    bands = mates * count
     for block in range(out_ref.shape[0]):
-        out_ref[block, 2:4, :lanes] = total
-        out_ref[block, 2:4, lanes:] = jnp.zeros((2, out_ref.shape[2] - lanes), F32)
+        out_ref[block, 2:4, :bands] = total[:, :bands]
+        out_ref[block, 2:4, bands:] = jnp.zeros((2, out_ref.shape[2] - bands), F32)
 
 
 def tail_kernel(mates, scale, recv_ref, sticks_ref, table_ref, out_hbm, corr_hbm, out_ref, corr_ref, sems):
@@ -252,11 +271,18 @@
     for part in own[1:]:
         total = total + part[2:4]
     total = total * scale
-    for q in range(corr_ref.shape[2] // mates):
+    side = side_of(mates)
+    count = corr_ref.shape[2] // mates
+    for q in range(count):
         for b in range(mates):
-            re, im, at = 8 * q + 2 * b, 8 * q + 2 * b + 1, q * mates + b
-            corr_ref[0, :, at : at + 1] = total[0:1, re : re + 1] + total[1:2, im : im + 1]
-            corr_ref[1, :, at : at + 1] = total[1:2, re : re + 1] - total[0:1, im : im + 1]
+            group, at = (b - q) % mates, q * mates + b
+            column = None
+            for k in range(mates):
+                row = (k - group) % mates * count + (q - lead_pair(group, mates)) % count
+                here = total[:, row : row + 1]
+                column = here if column is None else jnp.where(side == k, here, column)
+            for c in range(2):
+                corr_ref[c, :, at : at + 1] = column[c : c + 1]
     corr_copy = pltpu.make_async_copy(corr_ref, corr_hbm, sems.at[2])
     corr_copy.start()
     sphere = own_sphere(sticks_ref, stick_dev, box_edge)
@@ -288,9 +314,9 @@
     count = bands // mates
 
     send, *operands = pl.pallas_call(
-        functools.partial(head_kernel, mates),
+        functools.partial(head_kernel, count),
         out_shape=[
-            jax.ShapeDtypeStruct((mates * groups, 2, stick_dev), F32),
+            jax.ShapeDtypeStruct((count * groups, 2, stick_dev), F32),
             jax.ShapeDtypeStruct((box_edge, sticks), BF16),
             jax.ShapeDtypeStruct((box_edge, sticks), BF16),
             jax.ShapeDtypeStruct((grid_len, grid_len), BF16),
@@ -315,23 +341,33 @@
         in_hbm(fwd),
         in_hbm(transposed),
     )
-    order = [
-        [(q * mates + b) * groups + g for g in reversed(range(groups)) for b in reversed(range(mates))]
-        for q in range(count)
+    first = [
+        [
+            (q * mates + (side + q) % mates) * groups + g
+            for g in sorted(range(groups), key=lambda g: first_place(g, groups))
+            for q in [(lead_pair(side, mates) + t) % count for t in range(count)]
+        ]
+        for side in range(mates)
     ]
+    second = sorted(
+        ((g, b) for g in range(groups) for b in range(mates)), key=lambda member: place_of(*member, groups, mates)
+    )
+    second = [[(q * mates + b) * groups + g for g, b in second] for q in range(count)]
     planes = lax.all_to_all(
-        send, ("band", "pw"), split_axis=0, concat_axis=0, tiled=True, axis_index_groups=order
+        send, ("band", "pw"), split_axis=0, concat_axis=0, tiled=True, axis_index_groups=first
     )
     others = [
-        lax.ppermute(planes, "band", [(b, (b + s * mates) % bands) for b in range(bands)]) for s in range(1, count)
+        lax.ppermute(planes, "band", [(b, b - b % mates + (b + s) % mates) for b in range(bands)])
+        for s in range(1, mates)
     ]
+    span = -(-bands // 8) * 8
     blocks = jax.ShapeDtypeStruct((mates * groups, 4, stick_dev), F32)
     backs, rows, zeds = pl.pallas_call(
-        functools.partial(plane_kernel, mates),
+        functools.partial(plane_kernel, mates, count),
         out_shape=[
             blocks,
             jax.ShapeDtypeStruct((2, sticks), F32),
-            jax.ShapeDtypeStruct((8, sticks), F32),
+            jax.ShapeDtypeStruct((span, 2 * sticks), F32),
         ],
         in_specs=[vmem] * 6,
         out_specs=[vmem] * 3,
@@ -345,23 +381,22 @@
         cost_estimate=pl.CostEstimate(flops=1_400_000_000, bytes_accessed=3 << 20, transcendentals=0),
         name="plane",
     )(planes, *operands)
-    backs = pl.pallas_call(
+    backs, _ = pl.pallas_call(
         functools.partial(pair_kernel, mates, count),
-        out_shape=blocks,
-        in_specs=[vmem] * (2 + count),
-        out_specs=vmem,
-        scratch_shapes=[pltpu.VMEM((count, 8, sticks), F32)],
-        input_output_aliases={0: 0},
+        out_shape=[blocks, jax.ShapeDtypeStruct((span, 2 * sticks), F32)],
+        in_specs=[vmem] * (2 + mates),
+        out_specs=[vmem] * 2,
+        input_output_aliases={0: 0, 1: 1},
         compiler_params=pltpu.CompilerParams(vmem_limit_bytes=4 << 20),
         name="pairs",
-    )(backs, rows, zeds, *others)
+    )(backs, zeds, rows, *others)
     back = lax.all_to_all(
         backs,
         ("band", "pw"),
         split_axis=0,
         concat_axis=0,
         tiled=True,
-        axis_index_groups=order,
+        axis_index_groups=second,
     )
     applied, correlation = pl.pallas_call(
         functools.partial(tail_kernel, mates, 1.0 / math.sqrt(slab_len * sticks)),

time: 26 us -> 25.6 us (0.985)
  starting transfers between devices: 1.49 us -> 0.12 us
  blocking collectives: 18.8 us -> 19.9 us
    ppermute x1, starting transfers between devices: 1.49 us -> 0.12 us  [local(): lax.ppermute(planes, 'band', [(b, b - b % mates + (b + s) % mates) for b...]
    all_to_all x1, blocking collectives: 10.3 us -> 11.7 us  [local(): lax.all_to_all(send, ('band', 'pw'), split_axis=0, concat_axis=0, tiled=T...]
    all_to_all x1, blocking collectives: 8.48 us -> 8.19 us  [local(): lax.all_to_all(backs, ('band', 'pw'), split_axis=0, concat_axis=0, tiled=...]
where the time goes in v5:
time: 25.6 us; the launch traced here: 25.4 us
  blocking collectives  19.9 us (78%)
  Pallas kernels  4.69 us (18%)
  between operations  0.68 us (3%)
    all_to_all x1, blocking collectives, local(): lax.all_to_all(send, ('band', 'pw'), split_axis=0, concat_axis=0, tiled=T...  11.7 us
    all_to_all x1, blocking collectives, local(): lax.all_to_all(backs, ('band', 'pw'), split_axis=0, concat_axis=0, tiled=...  8.19 us
    pallas_call x1, Pallas kernels, local(): pl.pallas_call(functools.partial(plane_kernel, mates, count), out_shape=[...  2.25 us
    pallas_call x1, Pallas kernels, local(): pl.pallas_call(functools.partial(head_kernel, count), out_shape=[jax.Shap...  1.36 us
    pallas_call x1, Pallas kernels, local(): pl.pallas_call(functools.partial(tail_kernel, mates, 1.0 / math.sqrt(slab...  0.91 us
  transfers between devices with their start and end apart: 1, of which 0 were waited for; matrix products, arithmetic and copies ran while one was open for 0% of the time, Pallas kernels for 9%

profile of v5, /device:TPU:0, one launch (start us, length us, event | category | flops | bytes accessed | tf_op | source)
XLA Modules:
  0.0 25.4 jit_solution(2646167111754446460)
XLA Ops:
  0.6 1.4 %head.1 = (f32[16,2,128]{2,1,0:T(2,128)S(1)}, bf16[256,1024]{1,0:T(8,128)(2,1)S(1)}, bf16[256,1024]{1,0:T(8,128)(2,1)S(1)}, bf16[512,512]{1,0:T(8,128)(2,1)S(1)}...) custom-call(bf16[2,128,256]{2,1,0:T(8,128)(2,1)} %bitcast.10, s32[2,1024]{1,0:T(2,128)} %bitcast.7, ...), custom_call_target="tpu_custom_call" | custom-call | tf_op jit(solution)/shard_map/head/pallas_call | solution.py:316
  2.0 11.7 %all_to_all.10.recv_ref = f32[16,2,128]{2,1,0:T(2,128)S(1)} all-to-all(f32[16,2,128]{2,1,0:T(2,128)S(1)} %get-tuple-element.14), channel_id=1, replica_groups={{5,29,4,28,3,27,2,26,1,25,0,24,7,31,6,30},{21,13,20,12,19,11,18,10,17,9..., dimensions={0} | all-to-all | bytes 32768 | tf_op jit(solution)/shard_map/all_to_all | solution.py:356
  13.7 0.1 collective-permute-start
  13.8 2.2 %plane.1 = (f32[16,4,128]{2,1,0:T(4,128)S(1)}, f32[2,1024]{1,0:T(2,128)S(1)}, f32[8,2048]{1,0:T(8,128)S(1)}) custom-call(f32[16,2,128]{2,1,0:T(2,128)S(1)} %all_to_all.10.recv_ref, bf16[256,1024]{1,0:T(8,128)(2,1)S(1)} %get-tuple-element.15.hot_a, bf16[256,1024]{1,0:T(8,128)(2,1)S(1)} %get-tuple-element.16.hot_b, ...), custom_call_target="tpu_custom_call" | custom-call | flops 1400000000 | bytes 3145728 | tf_op jit(solution)/shard_map/plane/pallas_call | solution.py:365
  16.0 0.0 collective-permute-done.refs_0_
  16.1 0.2 pairs.1
  16.2 0.0 copy-start
  16.2 0.0 copy-start.1
  16.3 8.2 %all_to_all.11.recv_ref = f32[16,4,128]{2,1,0:T(4,128)S(1)} all-to-all(f32[16,4,128]{2,1,0:T(4,128)S(1)} %get-tuple-element.23), channel_id=1, replica_groups={{15,7,14,6,13,5,12,4,11,3,10,2,9,1,8,0},{31,23,30,22,29,21,28,20,27,19,..., dimensions={0} | all-to-all | bytes 65536 | tf_op jit(solution)/shard_map/all_to_all | solution.py:393
  24.4 0.0 copy-done
  24.4 0.0 copy-done.1
  24.5 0.9 %tail.1 = (bf16[2,128,256]{2,1,0:T(8,128)(2,1)}, f32[2,1,4]{2,1,0:T(1,128)}) custom-call(f32[16,4,128]{2,1,0:T(4,128)S(1)} %all_to_all.11.recv_ref, s32[2,1024]{1,0:T(2,128)S(1)} %bitcast.8, bf16[16,512]{1,0:T(8,128)(2,1)S(1)} %copy-done.1), custom_call_target="tpu_custom_call" | custom-call | tf_op jit(solution)/shard_map/tail/pallas_call | solution.py:401
Async XLA Ops:
  13.7 2.4 %collective-permute-start = (f32[16,2,128]{2,1,0:T(2,128)S(1)}, f32[16,2,128]{2,1,0:T(2,128)S(1)}, u32[]{:S(2)}, u32[]{:S(2)}) collective-permute-start(f32[16,2,128]{2,1,0:T(2,128)S(1)} %all_to_all.10.recv_ref), channel_id=1, source_target_pairs={{0,8},{8,0},{16,24},{24,16},{1,9},{9,1},{17,25},{25,17},{2,10},{10... | collective-permute-start | bytes 49160 | tf_op jit(solution)/shard_map/ppermute | solution.py:360
  16.2 8.2 %copy-start = (s32[1024,2]{0,1:T(2,128)S(1)}, s32[1024,2]{0,1:T(2,128)}, u32[]{:S(2)}) copy-start(s32[1024,2]{0,1:T(2,128)} %param.9) | copy-start | bytes 24580
  16.2 8.2 %copy-start.1 = (bf16[16,512]{1,0:T(8,128)(2,1)S(1)}, bf16[16,512]{1,0:T(8,128)(2,1)}, u32[]{:S(2)}) copy-start(bf16[16,512]{1,0:T(8,128)(2,1)} %constant.11.clone.table_ref) | copy-start | bytes 49156

commit v6 on v5

--- a/solution.py
+++ b/solution.py
@@ -150,11 +150,12 @@
     pot_ref,
     fwd_ref,
     tr_ref,
-    out_ref,
     back_ref,
     zeds_ref,
     spread,
     half_ref,
+    wide_ref,
+    left_ref,
     mid_ref,
     cell_ref,
 ):
@@ -176,60 +177,59 @@
                 spread[row : row + side, cols] = placed[p * side : (p + 1) * side]
 
     box = dot_nt(hot_a[...], spread[...]).astype(BF16)
-    even = dot_nn(box[:, :box_edge], fwd_ref[0])
-    odd = dot_nn(box[:, box_edge:], fwd_ref[1])
-    low = (even + odd).astype(BF16)
-    high = (even - odd).astype(BF16)
     for p in range(2):
-        rows = slice(p * side, (p + 1) * side)
-        for c in range(2):
-            cols = slice(c * n_half, (c + 1) * n_half)
-            half_ref[p, c * side : (c + 1) * side, :n_half] = low[rows, cols]
-            half_ref[p, c * side : (c + 1) * side, n_half:] = high[rows, cols]
-
-    step = 256
-    for x0 in range(0, n_half, step):
-        sums = {}
-        for c in range(2):
-            rows = slice(c * n_half + x0, c * n_half + x0 + step)
-            even = dot_nn(tr_ref[0, rows], half_ref[0])
-            odd = dot_nn(tr_ref[1, rows], half_ref[1])
-            near = (even + odd) * pot_ref[x0 : x0 + step].astype(F32)
-            far = (even - odd) * pot_ref[n_half + x0 : n_half + x0 + step].astype(F32)
+        wide_ref[p] = dot_nn(box[:, p * box_edge : (p + 1) * box_edge], fwd_ref[p])
+    for r in range(0, box_edge, 16):
+        even, odd = wide_ref[0, r : r + 16], wide_ref[1, r : r + 16]
+        p, at = r // side, r % side
+        for n, both in enumerate((even + odd, even - odd)):
+            both = both.astype(BF16)
+            for c in range(2):
+                half_ref[p, c * side + at : c * side + at + 16, n * n_half : (n + 1) * n_half] = both[
+                    :, c * n_half : (c + 1) * n_half
+                ]
+
+    for c in range(2):
+        for p in range(2):
+            wide_ref[2 * c + p] = dot_nn(tr_ref[p, c * n_half : (c + 1) * n_half], half_ref[p])
+    for c in range(2):
+        cols = slice(c * n_half, (c + 1) * n_half)
+        for r in range(0, n_half, 16):
+            rows = slice(r, r + 16)
+            even, odd = wide_ref[2 * c, rows], wide_ref[2 * c + 1, rows]
+            near = (even + odd) * pot_ref[rows].astype(F32)
+            far = (even - odd) * pot_ref[n_half + r : n_half + r + 16].astype(F32)
             for p, both in ((0, near + far), (1, near - far)):
-                sums[p, 0, c] = (both[:, :n_half] + both[:, n_half:]).astype(BF16)
-                sums[p, 1, c] = (both[:, :n_half] - both[:, n_half:]).astype(BF16)
-        for p in range(2):
-            for q in range(2):
-                left = jnp.concatenate([sums[p, q, 0], sums[p, q, 1]], axis=1)
-                mid = dot_nn(left, tr_ref[q]).astype(BF16)
-                for c in range(2):
-                    mid_ref[p, c * n_half + x0 : c * n_half + x0 + step, q * side : (q + 1) * side] = mid[
-                        :, c * side : (c + 1) * side
-                    ]
+                left_ref[p, 0, rows, cols] = (both[:, :n_half] + both[:, n_half:]).astype(BF16)
+                left_ref[p, 1, rows, cols] = (both[:, :n_half] - both[:, n_half:]).astype(BF16)
+    for p in range(2):
+        for q in range(2):
+            mid = dot_nn(left_ref[p, q], tr_ref[q]).astype(BF16)
+            for c in range(2):
+                mid_ref[p, c * n_half : (c + 1) * n_half, q * side : (q + 1) * side] = mid[
+                    :, c * side : (c + 1) * side
+                ]
 
     for p in range(2):
         cell = dot_nn(fwd_ref[p], mid_ref[p]) * (float(box_edge) / float(grid_len))
         cell_ref[p * box_edge : (p + 1) * box_edge] = cell.astype(BF16)
-
 
     wide = 256
     for s0 in range(0, sticks, wide):
         cols = slice(s0, s0 + wide)
         picked = dot_nn(cell_ref[...], hot_b[:, cols])
-        parts = []
-        for c in range(2):
-            value = None
-            for p in range(2):
-                at = p * box_edge + c * side
-                term = picked[at : at + side] * hot_a[p * side : (p + 1) * side, cols].astype(F32)
-                value = term if value is None else value + term
-            parts.append(jnp.sum(value, axis=0, keepdims=True))
+        parts = [None, None]
+        for p in range(2):
+            for r in range(0, side, 16):
+                hot = hot_a[p * side + r : p * side + r + 16, cols].astype(F32)
+                for c in range(2):
+                    at = p * box_edge + c * side + r
+                    term = picked[at : at + 16] * hot
+                    term = term[:8] + term[8:]
+                    parts[c] = term if parts[c] is None else parts[c] + term
+        parts = [jnp.sum(part, axis=0, keepdims=True) for part in parts]
         back = jnp.concatenate(parts, axis=0).astype(BF16).astype(F32)
         back_ref[:, cols] = back
-        for g in range(s0 // per, (s0 + wide) // per):
-            for b in range(mates):
-                out_ref[place_of(g, b, groups, mates), 0:2] = back[:, g * per - s0 : (g + 1) * per - s0]
     zeds_ref[...] = jnp.zeros_like(zeds_ref)
     gather_rows(count, 0, recv_ref, zeds_ref)
 
@@ -245,9 +245,9 @@
                 rows_ref[row : row + 1, at : at + per] = block[c : c + 1]
 
 
-def pair_kernel(mates, count, blocks_ref, seen_ref, back_ref, *refs):
+def pair_kernel(mates, count, seen_ref, back_ref, *refs):
     others, out_ref, zeds_ref = refs[: mates - 1], refs[mates - 1], refs[mates]
-    del blocks_ref, seen_ref
+    zeds_ref[...] = seen_ref[...]
     for s in range(1, mates):
         gather_rows(count, s, others[s - 1], zeds_ref)
     back = back_ref[...].astype(BF16)
@@ -256,9 +256,14 @@
     )
     total = dot_nt(left, zeds_ref[...].astype(BF16))
     bands = mates * count
-    for block in range(out_ref.shape[0]):
-        out_ref[block, 2:4, :bands] = total[:, :bands]
-        out_ref[block, 2:4, bands:] = jnp.zeros((2, out_ref.shape[2] - bands), F32)
+    blocks, _, per = out_ref.shape
+    groups = blocks // mates
+    for g in range(groups):
+        for b in range(mates):
+            at = place_of(g, b, groups, mates)
+            out_ref[at, 0:2] = back_ref[:, g * per : (g + 1) * per]
+            out_ref[at, 2:4, :bands] = total[:, :bands]
+            out_ref[at, 2:4, bands:] = jnp.zeros((2, per - bands), F32)
 
 
 def tail_kernel(mates, scale, recv_ref, sticks_ref, table_ref, out_hbm, corr_hbm, out_ref, corr_ref, sems):
@@ -361,19 +366,19 @@
         for s in range(1, mates)
     ]
     span = -(-bands // 8) * 8
-    blocks = jax.ShapeDtypeStruct((mates * groups, 4, stick_dev), F32)
-    backs, rows, zeds = pl.pallas_call(
+    rows, zeds = pl.pallas_call(
         functools.partial(plane_kernel, mates, count),
         out_shape=[
-            blocks,
             jax.ShapeDtypeStruct((2, sticks), F32),
             jax.ShapeDtypeStruct((span, 2 * sticks), F32),
         ],
         in_specs=[vmem] * 6,
-        out_specs=[vmem] * 3,
+        out_specs=[vmem] * 2,
         scratch_shapes=[
             pltpu.VMEM((2 * box_edge, sticks), BF16),
             pltpu.VMEM((2, box_edge, grid_len), BF16),
+            pltpu.VMEM((4, grid_len // 2, grid_len), F32),
+            pltpu.VMEM((2, 2, grid_len // 2, grid_len), BF16),
             pltpu.VMEM((2, grid_len, box_edge), BF16),
             pltpu.VMEM((2 * box_edge, box_edge), BF16),
         ],
@@ -381,15 +386,15 @@
         cost_estimate=pl.CostEstimate(flops=1_400_000_000, bytes_accessed=3 << 20, transcendentals=0),
         name="plane",
     )(planes, *operands)
-    backs, _ = pl.pallas_call(
+    backs = pl.pallas_call(
         functools.partial(pair_kernel, mates, count),
-        out_shape=[blocks, jax.ShapeDtypeStruct((span, 2 * sticks), F32)],
-        in_specs=[vmem] * (2 + mates),
-        out_specs=[vmem] * 2,
-        input_output_aliases={0: 0, 1: 1},
+        out_shape=jax.ShapeDtypeStruct((mates * groups, 4, stick_dev), F32),
+        in_specs=[vmem] * (1 + mates),
+        out_specs=vmem,
+        scratch_shapes=[pltpu.VMEM((span, 2 * sticks), F32)],
         compiler_params=pltpu.CompilerParams(vmem_limit_bytes=4 << 20),
         name="pairs",
-    )(backs, zeds, rows, *others)
+    )(zeds, rows, *others)
     back = lax.all_to_all(
         backs,
         ("band", "pw"),

time: 25.6 us -> 25.6 us (level)
  no operation moved by 1% of the time
where the time goes in v6:
time: 25.6 us; the launch traced here: 25.3 us
  blocking collectives  19.9 us (78%)
  Pallas kernels  4.62 us (18%)
  between operations  0.68 us (3%)
    all_to_all x1, blocking collectives, local(): lax.all_to_all(send, ('band', 'pw'), split_axis=0, concat_axis=0, tiled=T...  11.7 us
    all_to_all x1, blocking collectives, local(): lax.all_to_all(backs, ('band', 'pw'), split_axis=0, concat_axis=0, tiled=...  8.2 us
    pallas_call x1, Pallas kernels, local(): pl.pallas_call(functools.partial(plane_kernel, mates, count), out_shape=[...  2.18 us
    pallas_call x1, Pallas kernels, local(): pl.pallas_call(functools.partial(head_kernel, count), out_shape=[jax.Shap...  1.36 us
    pallas_call x1, Pallas kernels, local(): pl.pallas_call(functools.partial(tail_kernel, mates, 1.0 / math.sqrt(slab...  0.91 us
  transfers between devices with their start and end apart: 1, of which 0 were waited for; matrix products, arithmetic and copies ran while one was open for 0% of the time, Pallas kernels for 9%

profile of v6, /device:TPU:0, one launch (start us, length us, event | category | flops | bytes accessed | tf_op | source)
XLA Modules:
  0.0 25.3 jit_solution(11476046627622252717)
XLA Ops:
  0.6 1.4 %head.1 = (f32[16,2,128]{2,1,0:T(2,128)S(1)}, bf16[256,1024]{1,0:T(8,128)(2,1)S(1)}, bf16[256,1024]{1,0:T(8,128)(2,1)S(1)}, bf16[512,512]{1,0:T(8,128)(2,1)S(1)}...) custom-call(bf16[2,128,256]{2,1,0:T(8,128)(2,1)} %bitcast.10, s32[2,1024]{1,0:T(2,128)} %bitcast.7, ...), custom_call_target="tpu_custom_call" | custom-call | tf_op jit(solution)/shard_map/head/pallas_call | solution.py:321
  2.0 11.7 %all_to_all.10.recv_ref = f32[16,2,128]{2,1,0:T(2,128)S(1)} all-to-all(f32[16,2,128]{2,1,0:T(2,128)S(1)} %get-tuple-element.12), channel_id=1, replica_groups={{5,29,4,28,3,27,2,26,1,25,0,24,7,31,6,30},{21,13,20,12,19,11,18,10,17,9..., dimensions={0} | all-to-all | bytes 32768 | tf_op jit(solution)/shard_map/all_to_all | solution.py:361
  13.7 0.1 collective-permute-start
  13.8 2.2 %plane.1 = (f32[2,1024]{1,0:T(2,128)S(1)}, f32[8,2048]{1,0:T(8,128)S(1)}) custom-call(f32[16,2,128]{2,1,0:T(2,128)S(1)} %all_to_all.10.recv_ref, bf16[256,1024]{1,0:T(8,128)(2,1)S(1)} %get-tuple-element.13.hot_a, bf16[256,1024]{1,0:T(8,128)(2,1)S(1)} %get-tuple-element.14.hot_b, bf16[512,512]{1,0:T(8,128)(2,1)S(1)} %get-tuple-element.15.pot_ref, ...), custom_call_target="tpu_custom_call" | custom-call | flops 1400000000 | bytes 3145728 | tf_op jit(solution)/shard_map/plane/pallas_call | solution.py:369
  16.0 0.0 collective-permute-done.refs_0_
  16.0 0.2 pairs.1
  16.2 0.0 copy-start
  16.2 0.0 copy-start.1
  16.2 8.2 %all_to_all.11.recv_ref = f32[16,4,128]{2,1,0:T(4,128)S(1)} all-to-all(f32[16,4,128]{2,1,0:T(4,128)S(1)} %pairs.1), channel_id=1, replica_groups={{15,7,14,6,13,5,12,4,11,3,10,2,9,1,8,0},{31,23,30,22,29,21,28,20,27,19,..., dimensions={0} | all-to-all | bytes 65536 | tf_op jit(solution)/shard_map/all_to_all | solution.py:398
  24.4 0.0 copy-done
  24.4 0.0 copy-done.1
  24.4 0.9 %tail.1 = (bf16[2,128,256]{2,1,0:T(8,128)(2,1)}, f32[2,1,4]{2,1,0:T(1,128)}) custom-call(f32[16,4,128]{2,1,0:T(4,128)S(1)} %all_to_all.11.recv_ref, s32[2,1024]{1,0:T(2,128)S(1)} %bitcast.8, bf16[16,512]{1,0:T(8,128)(2,1)S(1)} %copy-done.1), custom_call_target="tpu_custom_call" | custom-call | tf_op jit(solution)/shard_map/tail/pallas_call | solution.py:406
Async XLA Ops:
  13.7 2.3 %collective-permute-start = (f32[16,2,128]{2,1,0:T(2,128)S(1)}, f32[16,2,128]{2,1,0:T(2,128)S(1)}, u32[]{:S(2)}, u32[]{:S(2)}) collective-permute-start(f32[16,2,128]{2,1,0:T(2,128)S(1)} %all_to_all.10.recv_ref), channel_id=1, source_target_pairs={{0,8},{8,0},{16,24},{24,16},{1,9},{9,1},{17,25},{25,17},{2,10},{10... | collective-permute-start | bytes 49160 | tf_op jit(solution)/shard_map/ppermute | solution.py:365
  16.2 8.2 %copy-start = (s32[1024,2]{0,1:T(2,128)S(1)}, s32[1024,2]{0,1:T(2,128)}, u32[]{:S(2)}) copy-start(s32[1024,2]{0,1:T(2,128)} %param.9) | copy-start | bytes 24580
  16.2 8.2 %copy-start.1 = (bf16[16,512]{1,0:T(8,128)(2,1)S(1)}, bf16[16,512]{1,0:T(8,128)(2,1)}, u32[]{:S(2)}) copy-start(bf16[16,512]{1,0:T(8,128)(2,1)} %constant.11.clone.table_ref) | copy-start | bytes 49156

commit v7 on v6

--- a/solution.py
+++ b/solution.py
@@ -108,8 +108,8 @@
         (pot_hbm, pot_ref),
     ]
     copies = [pltpu.make_async_copy(src, dst, sems.at[n]) for n, (src, dst) in enumerate(pairs)]
-    for copy in copies:
-        copy.start()
+    for n, copy in enumerate(copies):
+        copy.start(priority=n // 3)
     _, stick_dev, box_edge = coeffs_ref.shape
     slab_len = table_ref.shape[0] // 2
     copies[0].wait()

time: 25.6 us -> 25.6 us (level)
  no operation moved by 1% of the time
where the time goes in v7:
time: 25.6 us; the launch traced here: 25.3 us
  blocking collectives  19.9 us (78%)
  Pallas kernels  4.62 us (18%)
  between operations  0.68 us (3%)
    all_to_all x1, blocking collectives, local(): lax.all_to_all(send, ('band', 'pw'), split_axis=0, concat_axis=0, tiled=T...  11.7 us
    all_to_all x1, blocking collectives, local(): lax.all_to_all(backs, ('band', 'pw'), split_axis=0, concat_axis=0, tiled=...  8.19 us
    pallas_call x1, Pallas kernels, local(): pl.pallas_call(functools.partial(plane_kernel, mates, count), out_shape=[...  2.19 us
    pallas_call x1, Pallas kernels, local(): pl.pallas_call(functools.partial(head_kernel, count), out_shape=[jax.Shap...  1.35 us
    pallas_call x1, Pallas kernels, local(): pl.pallas_call(functools.partial(tail_kernel, mates, 1.0 / math.sqrt(slab...  0.91 us
  transfers between devices with their start and end apart: 1, of which 0 were waited for; matrix products, arithmetic and copies ran while one was open for 0% of the time, Pallas kernels for 9%

profile of v7, /device:TPU:0, one launch (start us, length us, event | category | flops | bytes accessed | tf_op | source)
XLA Modules:
  0.0 25.3 jit_solution(16330467107105787259)
XLA Ops:
  0.6 1.4 %head.1 = (f32[16,2,128]{2,1,0:T(2,128)S(1)}, bf16[256,1024]{1,0:T(8,128)(2,1)S(1)}, bf16[256,1024]{1,0:T(8,128)(2,1)S(1)}, bf16[512,512]{1,0:T(8,128)(2,1)S(1)}...) custom-call(bf16[2,128,256]{2,1,0:T(8,128)(2,1)} %bitcast.10, s32[2,1024]{1,0:T(2,128)} %bitcast.7, ...), custom_call_target="tpu_custom_call" | custom-call | tf_op jit(solution)/shard_map/head/pallas_call | solution.py:321
  2.0 11.7 %all_to_all.10.recv_ref = f32[16,2,128]{2,1,0:T(2,128)S(1)} all-to-all(f32[16,2,128]{2,1,0:T(2,128)S(1)} %get-tuple-element.12), channel_id=1, replica_groups={{5,29,4,28,3,27,2,26,1,25,0,24,7,31,6,30},{21,13,20,12,19,11,18,10,17,9..., dimensions={0} | all-to-all | bytes 32768 | tf_op jit(solution)/shard_map/all_to_all | solution.py:361
  13.7 0.1 collective-permute-start
  13.8 2.2 %plane.1 = (f32[2,1024]{1,0:T(2,128)S(1)}, f32[8,2048]{1,0:T(8,128)S(1)}) custom-call(f32[16,2,128]{2,1,0:T(2,128)S(1)} %all_to_all.10.recv_ref, bf16[256,1024]{1,0:T(8,128)(2,1)S(1)} %get-tuple-element.13.hot_a, bf16[256,1024]{1,0:T(8,128)(2,1)S(1)} %get-tuple-element.14.hot_b, bf16[512,512]{1,0:T(8,128)(2,1)S(1)} %get-tuple-element.15.pot_ref, ...), custom_call_target="tpu_custom_call" | custom-call | flops 1400000000 | bytes 3145728 | tf_op jit(solution)/shard_map/plane/pallas_call | solution.py:369
  16.0 0.0 collective-permute-done.refs_0_
  16.0 0.2 pairs.1
  16.2 0.0 copy-start
  16.2 0.0 copy-start.1
  16.2 8.2 %all_to_all.11.recv_ref = f32[16,4,128]{2,1,0:T(4,128)S(1)} all-to-all(f32[16,4,128]{2,1,0:T(4,128)S(1)} %pairs.1), channel_id=1, replica_groups={{15,7,14,6,13,5,12,4,11,3,10,2,9,1,8,0},{31,23,30,22,29,21,28,20,27,19,..., dimensions={0} | all-to-all | bytes 65536 | tf_op jit(solution)/shard_map/all_to_all | solution.py:398
  24.4 0.0 copy-done
  24.4 0.0 copy-done.1
  24.4 0.9 %tail.1 = (bf16[2,128,256]{2,1,0:T(8,128)(2,1)}, f32[2,1,4]{2,1,0:T(1,128)}) custom-call(f32[16,4,128]{2,1,0:T(4,128)S(1)} %all_to_all.11.recv_ref, s32[2,1024]{1,0:T(2,128)S(1)} %bitcast.8, bf16[16,512]{1,0:T(8,128)(2,1)S(1)} %copy-done.1), custom_call_target="tpu_custom_call" | custom-call | tf_op jit(solution)/shard_map/tail/pallas_call | solution.py:406
Async XLA Ops:
  13.7 2.3 %collective-permute-start = (f32[16,2,128]{2,1,0:T(2,128)S(1)}, f32[16,2,128]{2,1,0:T(2,128)S(1)}, u32[]{:S(2)}, u32[]{:S(2)}) collective-permute-start(f32[16,2,128]{2,1,0:T(2,128)S(1)} %all_to_all.10.recv_ref), channel_id=1, source_target_pairs={{0,8},{8,0},{16,24},{24,16},{1,9},{9,1},{17,25},{25,17},{2,10},{10... | collective-permute-start | bytes 49160 | tf_op jit(solution)/shard_map/ppermute | solution.py:365
  16.2 8.2 %copy-start = (s32[1024,2]{0,1:T(2,128)S(1)}, s32[1024,2]{0,1:T(2,128)}, u32[]{:S(2)}) copy-start(s32[1024,2]{0,1:T(2,128)} %param.9) | copy-start | bytes 24580
  16.2 8.2 %copy-start.1 = (bf16[16,512]{1,0:T(8,128)(2,1)S(1)}, bf16[16,512]{1,0:T(8,128)(2,1)}, u32[]{:S(2)}) copy-start(bf16[16,512]{1,0:T(8,128)(2,1)} %constant.11.clone.table_ref) | copy-start | bytes 49156

commit v8 on v7

--- a/solution.py
+++ b/solution.py
@@ -192,13 +192,15 @@
     for c in range(2):
         for p in range(2):
             wide_ref[2 * c + p] = dot_nn(tr_ref[p, c * n_half : (c + 1) * n_half], half_ref[p])
-    for c in range(2):
-        cols = slice(c * n_half, (c + 1) * n_half)
-        for r in range(0, n_half, 16):
-            rows = slice(r, r + 16)
+    for r in range(0, n_half, 16):
+        rows = slice(r, r + 16)
+        pot_near = pot_ref[rows].astype(F32)
+        pot_far = pot_ref[n_half + r : n_half + r + 16].astype(F32)
+        for c in range(2):
+            cols = slice(c * n_half, (c + 1) * n_half)
             even, odd = wide_ref[2 * c, rows], wide_ref[2 * c + 1, rows]
-            near = (even + odd) * pot_ref[rows].astype(F32)
-            far = (even - odd) * pot_ref[n_half + r : n_half + r + 16].astype(F32)
+            near = (even + odd) * pot_near
+            far = (even - odd) * pot_far
             for p, both in ((0, near + far), (1, near - far)):
                 left_ref[p, 0, rows, cols] = (both[:, :n_half] + both[:, n_half:]).astype(BF16)
                 left_ref[p, 1, rows, cols] = (both[:, :n_half] - both[:, n_half:]).astype(BF16)
@@ -211,8 +213,7 @@
                 ]
 
     for p in range(2):
-        cell = dot_nn(fwd_ref[p], mid_ref[p]) * (float(box_edge) / float(grid_len))
-        cell_ref[p * box_edge : (p + 1) * box_edge] = cell.astype(BF16)
+        cell_ref[p * box_edge : (p + 1) * box_edge] = dot_nn(fwd_ref[p], mid_ref[p]).astype(BF16)
 
     wide = 256
     for s0 in range(0, sticks, wide):
@@ -228,8 +229,8 @@
                     term = term[:8] + term[8:]
                     parts[c] = term if parts[c] is None else parts[c] + term
         parts = [jnp.sum(part, axis=0, keepdims=True) for part in parts]
-        back = jnp.concatenate(parts, axis=0).astype(BF16).astype(F32)
-        back_ref[:, cols] = back
+        back = jnp.concatenate(parts, axis=0) * (float(box_edge) / float(grid_len))
+        back_ref[:, cols] = back.astype(BF16).astype(F32)
     zeds_ref[...] = jnp.zeros_like(zeds_ref)
     gather_rows(count, 0, recv_ref, zeds_ref)
 
@@ -289,7 +290,7 @@
             for c in range(2):
                 corr_ref[c, :, at : at + 1] = column[c : c + 1]
     corr_copy = pltpu.make_async_copy(corr_ref, corr_hbm, sems.at[2])
-    corr_copy.start()
+    corr_copy.start(priority=1)
     sphere = own_sphere(sticks_ref, stick_dev, box_edge)
     back = jnp.concatenate([part[c : c + 1] for c in range(2) for part in own], axis=0).astype(BF16)
     copies = []
@@ -297,7 +298,7 @@
         values = dot_tn(back, table_ref[:, c * box_edge : (c + 1) * box_edge])
         out_ref[c] = jnp.where(sphere, values, 0.0).astype(BF16)
         copies.append(pltpu.make_async_copy(out_ref.at[c], out_hbm.at[c], sems.at[c]))
-        copies[-1].start()
+        copies[-1].start(priority=c)
     for copy in copies:
         copy.wait()
     corr_copy.wait()

time: 25.6 us -> 25.6 us (level)
  no operation moved by 1% of the time
where the time goes in v8:
time: 25.6 us; the launch traced here: 25.3 us
  blocking collectives  19.9 us (78%)
  Pallas kernels  4.64 us (18%)
  between operations  0.68 us (3%)
    all_to_all x1, blocking collectives, local(): lax.all_to_all(send, ('band', 'pw'), split_axis=0, concat_axis=0, tiled=T...  11.7 us
    all_to_all x1, blocking collectives, local(): lax.all_to_all(backs, ('band', 'pw'), split_axis=0, concat_axis=0, tiled=...  8.19 us
    pallas_call x1, Pallas kernels, local(): pl.pallas_call(functools.partial(plane_kernel, mates, count), out_shape=[...  2.21 us
    pallas_call x1, Pallas kernels, local(): pl.pallas_call(functools.partial(head_kernel, count), out_shape=[jax.Shap...  1.35 us
    pallas_call x1, Pallas kernels, local(): pl.pallas_call(functools.partial(tail_kernel, mates, 1.0 / math.sqrt(slab...  0.91 us
  transfers between devices with their start and end apart: 1, of which 0 were waited for; matrix products, arithmetic and copies ran while one was open for 0% of the time, Pallas kernels for 9%

profile of v8, /device:TPU:0, one launch (start us, length us, event | category | flops | bytes accessed | tf_op | source)
XLA Modules:
  0.0 25.3 jit_solution(17114711287766618306)
XLA Ops:
  0.6 1.4 %head.1 = (f32[16,2,128]{2,1,0:T(2,128)S(1)}, bf16[256,1024]{1,0:T(8,128)(2,1)S(1)}, bf16[256,1024]{1,0:T(8,128)(2,1)S(1)}, bf16[512,512]{1,0:T(8,128)(2,1)S(1)}...) custom-call(bf16[2,128,256]{2,1,0:T(8,128)(2,1)} %bitcast.10, s32[2,1024]{1,0:T(2,128)} %bitcast.7, ...), custom_call_target="tpu_custom_call" | custom-call | tf_op jit(solution)/shard_map/head/pallas_call | solution.py:322
  2.0 11.7 %all_to_all.10.recv_ref = f32[16,2,128]{2,1,0:T(2,128)S(1)} all-to-all(f32[16,2,128]{2,1,0:T(2,128)S(1)} %get-tuple-element.12), channel_id=1, replica_groups={{5,29,4,28,3,27,2,26,1,25,0,24,7,31,6,30},{21,13,20,12,19,11,18,10,17,9..., dimensions={0} | all-to-all | bytes 32768 | tf_op jit(solution)/shard_map/all_to_all | solution.py:362
  13.7 0.1 collective-permute-start
  13.8 2.2 %plane.1 = (f32[2,1024]{1,0:T(2,128)S(1)}, f32[8,2048]{1,0:T(8,128)S(1)}) custom-call(f32[16,2,128]{2,1,0:T(2,128)S(1)} %all_to_all.10.recv_ref, bf16[256,1024]{1,0:T(8,128)(2,1)S(1)} %get-tuple-element.13.hot_a, bf16[256,1024]{1,0:T(8,128)(2,1)S(1)} %get-tuple-element.14.hot_b, bf16[512,512]{1,0:T(8,128)(2,1)S(1)} %get-tuple-element.15.pot_ref, ...), custom_call_target="tpu_custom_call" | custom-call | flops 1400000000 | bytes 3145728 | tf_op jit(solution)/shard_map/plane/pallas_call | solution.py:370
  16.0 0.0 collective-permute-done.refs_0_
  16.0 0.2 pairs.1
  16.2 0.0 copy-start
  16.2 0.0 copy-start.1
  16.2 8.2 %all_to_all.11.recv_ref = f32[16,4,128]{2,1,0:T(4,128)S(1)} all-to-all(f32[16,4,128]{2,1,0:T(4,128)S(1)} %pairs.1), channel_id=1, replica_groups={{15,7,14,6,13,5,12,4,11,3,10,2,9,1,8,0},{31,23,30,22,29,21,28,20,27,19,..., dimensions={0} | all-to-all | bytes 65536 | tf_op jit(solution)/shard_map/all_to_all | solution.py:399
  24.4 0.0 copy-done
  24.4 0.0 copy-done.1
  24.4 0.9 %tail.1 = (bf16[2,128,256]{2,1,0:T(8,128)(2,1)}, f32[2,1,4]{2,1,0:T(1,128)}) custom-call(f32[16,4,128]{2,1,0:T(4,128)S(1)} %all_to_all.11.recv_ref, s32[2,1024]{1,0:T(2,128)S(1)} %bitcast.8, bf16[16,512]{1,0:T(8,128)(2,1)S(1)} %copy-done.1), custom_call_target="tpu_custom_call" | custom-call | tf_op jit(solution)/shard_map/tail/pallas_call | solution.py:407
Async XLA Ops:
  13.7 2.3 %collective-permute-start = (f32[16,2,128]{2,1,0:T(2,128)S(1)}, f32[16,2,128]{2,1,0:T(2,128)S(1)}, u32[]{:S(2)}, u32[]{:S(2)}) collective-permute-start(f32[16,2,128]{2,1,0:T(2,128)S(1)} %all_to_all.10.recv_ref), channel_id=1, source_target_pairs={{0,8},{8,0},{16,24},{24,16},{1,9},{9,1},{17,25},{25,17},{2,10},{10... | collective-permute-start | bytes 49160 | tf_op jit(solution)/shard_map/ppermute | solution.py:366
  16.2 8.2 %copy-start = (s32[1024,2]{0,1:T(2,128)S(1)}, s32[1024,2]{0,1:T(2,128)}, u32[]{:S(2)}) copy-start(s32[1024,2]{0,1:T(2,128)} %param.9) | copy-start | bytes 24580
  16.2 8.2 %copy-start.1 = (bf16[16,512]{1,0:T(8,128)(2,1)S(1)}, bf16[16,512]{1,0:T(8,128)(2,1)}, u32[]{:S(2)}) copy-start(bf16[16,512]{1,0:T(8,128)(2,1)} %constant.11.clone.table_ref) | copy-start | bytes 49156

commit v9 on v8

--- a/solution.py
+++ b/solution.py
@@ -101,21 +101,21 @@
     side, n_half = fwd_hbm.shape[1], tr_hbm.shape[1]
     pairs = [
         (sticks_hbm, sticks_ref),
+        (table_hbm, table_ref),
         (coeffs_hbm, coeffs_ref),
-        (table_hbm, table_ref),
         (fwd_hbm, fwd_ref.at[:, :side]),
         (tr_hbm, tr_ref.at[:, :n_half]),
         (pot_hbm, pot_ref),
     ]
     copies = [pltpu.make_async_copy(src, dst, sems.at[n]) for n, (src, dst) in enumerate(pairs)]
     for n, copy in enumerate(copies):
-        copy.start(priority=n // 3)
+        copy.start(priority=int(n not in (0, 2)))
     _, stick_dev, box_edge = coeffs_ref.shape
     slab_len = table_ref.shape[0] // 2
     copies[0].wait()
     sphere = own_sphere(sticks_ref, stick_dev, box_edge)
+    copies[2].wait()
     copies[1].wait()
-    copies[2].wait()
     masked = [jnp.where(sphere, coeffs_ref[c].astype(F32), 0.0).astype(BF16) for c in range(2)]
     masked = jnp.concatenate(masked, axis=1)
     rows = dot_nt(table_ref[...], masked).astype(BF16).astype(F32)

time: 25.6 us -> 25.6 us (level)
  no operation moved by 1% of the time
where the time goes in v9:
time: 25.6 us; the launch traced here: 25.3 us
  blocking collectives  19.9 us (78%)
  Pallas kernels  4.64 us (18%)
  between operations  0.68 us (3%)
    all_to_all x1, blocking collectives, local(): lax.all_to_all(send, ('band', 'pw'), split_axis=0, concat_axis=0, tiled=T...  11.7 us
    all_to_all x1, blocking collectives, local(): lax.all_to_all(backs, ('band', 'pw'), split_axis=0, concat_axis=0, tiled=...  8.19 us
    pallas_call x1, Pallas kernels, local(): pl.pallas_call(functools.partial(plane_kernel, mates, count), out_shape=[...  2.21 us
    pallas_call x1, Pallas kernels, local(): pl.pallas_call(functools.partial(head_kernel, count), out_shape=[jax.Shap...  1.35 us
    pallas_call x1, Pallas kernels, local(): pl.pallas_call(functools.partial(tail_kernel, mates, 1.0 / math.sqrt(slab...  0.91 us
  transfers between devices with their start and end apart: 1, of which 0 were waited for; matrix products, arithmetic and copies ran while one was open for 0% of the time, Pallas kernels for 9%

profile of v9, /device:TPU:0, one launch (start us, length us, event | category | flops | bytes accessed | tf_op | source)
XLA Modules:
  0.0 25.3 jit_solution(7141119121165703439)
XLA Ops:
  0.6 1.4 %head.1 = (f32[16,2,128]{2,1,0:T(2,128)S(1)}, bf16[256,1024]{1,0:T(8,128)(2,1)S(1)}, bf16[256,1024]{1,0:T(8,128)(2,1)S(1)}, bf16[512,512]{1,0:T(8,128)(2,1)S(1)}...) custom-call(bf16[2,128,256]{2,1,0:T(8,128)(2,1)} %bitcast.10, s32[2,1024]{1,0:T(2,128)} %bitcast.7, ...), custom_call_target="tpu_custom_call" | custom-call | tf_op jit(solution)/shard_map/head/pallas_call | solution.py:322
  2.0 11.7 %all_to_all.10.recv_ref = f32[16,2,128]{2,1,0:T(2,128)S(1)} all-to-all(f32[16,2,128]{2,1,0:T(2,128)S(1)} %get-tuple-element.12), channel_id=1, replica_groups={{5,29,4,28,3,27,2,26,1,25,0,24,7,31,6,30},{21,13,20,12,19,11,18,10,17,9..., dimensions={0} | all-to-all | bytes 32768 | tf_op jit(solution)/shard_map/all_to_all | solution.py:362
  13.7 0.1 collective-permute-start
  13.8 2.2 %plane.1 = (f32[2,1024]{1,0:T(2,128)S(1)}, f32[8,2048]{1,0:T(8,128)S(1)}) custom-call(f32[16,2,128]{2,1,0:T(2,128)S(1)} %all_to_all.10.recv_ref, bf16[256,1024]{1,0:T(8,128)(2,1)S(1)} %get-tuple-element.13.hot_a, bf16[256,1024]{1,0:T(8,128)(2,1)S(1)} %get-tuple-element.14.hot_b, bf16[512,512]{1,0:T(8,128)(2,1)S(1)} %get-tuple-element.15.pot_ref, ...), custom_call_target="tpu_custom_call" | custom-call | flops 1400000000 | bytes 3145728 | tf_op jit(solution)/shard_map/plane/pallas_call | solution.py:370
  16.0 0.0 collective-permute-done.refs_0_
  16.0 0.2 pairs.1
  16.2 0.0 copy-start
  16.2 0.0 copy-start.1
  16.2 8.2 %all_to_all.11.recv_ref = f32[16,4,128]{2,1,0:T(4,128)S(1)} all-to-all(f32[16,4,128]{2,1,0:T(4,128)S(1)} %pairs.1), channel_id=1, replica_groups={{15,7,14,6,13,5,12,4,11,3,10,2,9,1,8,0},{31,23,30,22,29,21,28,20,27,19,..., dimensions={0} | all-to-all | bytes 65536 | tf_op jit(solution)/shard_map/all_to_all | solution.py:399
  24.4 0.0 copy-done
  24.4 0.0 copy-done.1
  24.4 0.9 %tail.1 = (bf16[2,128,256]{2,1,0:T(8,128)(2,1)}, f32[2,1,4]{2,1,0:T(1,128)}) custom-call(f32[16,4,128]{2,1,0:T(4,128)S(1)} %all_to_all.11.recv_ref, s32[2,1024]{1,0:T(2,128)S(1)} %bitcast.8, bf16[16,512]{1,0:T(8,128)(2,1)S(1)} %copy-done.1), custom_call_target="tpu_custom_call" | custom-call | tf_op jit(solution)/shard_map/tail/pallas_call | solution.py:407
Async XLA Ops:
  13.7 2.3 %collective-permute-start = (f32[16,2,128]{2,1,0:T(2,128)S(1)}, f32[16,2,128]{2,1,0:T(2,128)S(1)}, u32[]{:S(2)}, u32[]{:S(2)}) collective-permute-start(f32[16,2,128]{2,1,0:T(2,128)S(1)} %all_to_all.10.recv_ref), channel_id=1, source_target_pairs={{0,8},{8,0},{16,24},{24,16},{1,9},{9,1},{17,25},{25,17},{2,10},{10... | collective-permute-start | bytes 49160 | tf_op jit(solution)/shard_map/ppermute | solution.py:366
  16.2 8.2 %copy-start = (s32[1024,2]{0,1:T(2,128)S(1)}, s32[1024,2]{0,1:T(2,128)}, u32[]{:S(2)}) copy-start(s32[1024,2]{0,1:T(2,128)} %param.9) | copy-start | bytes 24580
  16.2 8.2 %copy-start.1 = (bf16[16,512]{1,0:T(8,128)(2,1)S(1)}, bf16[16,512]{1,0:T(8,128)(2,1)}, u32[]{:S(2)}) copy-start(bf16[16,512]{1,0:T(8,128)(2,1)} %constant.11.clone.table_ref) | copy-start | bytes 49156

commit v10 on v9

--- a/solution.py
+++ b/solution.py
@@ -206,7 +206,7 @@
                 left_ref[p, 1, rows, cols] = (both[:, :n_half] - both[:, n_half:]).astype(BF16)
     for p in range(2):
         for q in range(2):
-            mid = dot_nn(left_ref[p, q], tr_ref[q]).astype(BF16)
+            mid = dot_nt(left_ref[p, q], fwd_ref[q]).astype(BF16)
             for c in range(2):
                 mid_ref[p, c * n_half : (c + 1) * n_half, q * side : (q + 1) * side] = mid[
                     :, c * side : (c + 1) * side

time: 25.6 us -> 25.6 us (level)
  no operation moved by 1% of the time
where the time goes in v10:
time: 25.6 us; the launch traced here: 25.3 us
  blocking collectives  19.9 us (78%)
  Pallas kernels  4.65 us (18%)
  between operations  0.68 us (3%)
    all_to_all x1, blocking collectives, local(): lax.all_to_all(send, ('band', 'pw'), split_axis=0, concat_axis=0, tiled=T...  11.7 us
    all_to_all x1, blocking collectives, local(): lax.all_to_all(backs, ('band', 'pw'), split_axis=0, concat_axis=0, tiled=...  8.19 us
    pallas_call x1, Pallas kernels, local(): pl.pallas_call(functools.partial(plane_kernel, mates, count), out_shape=[...  2.22 us
    pallas_call x1, Pallas kernels, local(): pl.pallas_call(functools.partial(head_kernel, count), out_shape=[jax.Shap...  1.35 us
    pallas_call x1, Pallas kernels, local(): pl.pallas_call(functools.partial(tail_kernel, mates, 1.0 / math.sqrt(slab...  0.91 us
  transfers between devices with their start and end apart: 1, of which 0 were waited for; matrix products, arithmetic and copies ran while one was open for 0% of the time, Pallas kernels for 9%

profile of v10, /device:TPU:0, one launch (start us, length us, event | category | flops | bytes accessed | tf_op | source)
XLA Modules:
  0.0 25.3 jit_solution(18431620356822959516)
XLA Ops:
  0.6 1.4 %head.1 = (f32[16,2,128]{2,1,0:T(2,128)S(1)}, bf16[256,1024]{1,0:T(8,128)(2,1)S(1)}, bf16[256,1024]{1,0:T(8,128)(2,1)S(1)}, bf16[512,512]{1,0:T(8,128)(2,1)S(1)}...) custom-call(bf16[2,128,256]{2,1,0:T(8,128)(2,1)} %bitcast.10, s32[2,1024]{1,0:T(2,128)} %bitcast.7, ...), custom_call_target="tpu_custom_call" | custom-call | tf_op jit(solution)/shard_map/head/pallas_call | solution.py:322
  2.0 11.7 %all_to_all.10.recv_ref = f32[16,2,128]{2,1,0:T(2,128)S(1)} all-to-all(f32[16,2,128]{2,1,0:T(2,128)S(1)} %get-tuple-element.12), channel_id=1, replica_groups={{5,29,4,28,3,27,2,26,1,25,0,24,7,31,6,30},{21,13,20,12,19,11,18,10,17,9..., dimensions={0} | all-to-all | bytes 32768 | tf_op jit(solution)/shard_map/all_to_all | solution.py:362
  13.7 0.1 collective-permute-start
  13.8 2.2 %plane.1 = (f32[2,1024]{1,0:T(2,128)S(1)}, f32[8,2048]{1,0:T(8,128)S(1)}) custom-call(f32[16,2,128]{2,1,0:T(2,128)S(1)} %all_to_all.10.recv_ref, bf16[256,1024]{1,0:T(8,128)(2,1)S(1)} %get-tuple-element.13.hot_a, bf16[256,1024]{1,0:T(8,128)(2,1)S(1)} %get-tuple-element.14.hot_b, bf16[512,512]{1,0:T(8,128)(2,1)S(1)} %get-tuple-element.15.pot_ref, ...), custom_call_target="tpu_custom_call" | custom-call | flops 1400000000 | bytes 3145728 | tf_op jit(solution)/shard_map/plane/pallas_call | solution.py:370
  16.0 0.0 collective-permute-done.refs_0_
  16.0 0.2 pairs.1
  16.2 0.0 copy-start
  16.2 0.0 copy-start.1
  16.2 8.2 %all_to_all.11.recv_ref = f32[16,4,128]{2,1,0:T(4,128)S(1)} all-to-all(f32[16,4,128]{2,1,0:T(4,128)S(1)} %pairs.1), channel_id=1, replica_groups={{15,7,14,6,13,5,12,4,11,3,10,2,9,1,8,0},{31,23,30,22,29,21,28,20,27,19,..., dimensions={0} | all-to-all | bytes 65536 | tf_op jit(solution)/shard_map/all_to_all | solution.py:399
  24.4 0.0 copy-done
  24.4 0.0 copy-done.1
  24.4 0.9 %tail.1 = (bf16[2,128,256]{2,1,0:T(8,128)(2,1)}, f32[2,1,4]{2,1,0:T(1,128)}) custom-call(f32[16,4,128]{2,1,0:T(4,128)S(1)} %all_to_all.11.recv_ref, s32[2,1024]{1,0:T(2,128)S(1)} %bitcast.8, bf16[16,512]{1,0:T(8,128)(2,1)S(1)} %copy-done.1), custom_call_target="tpu_custom_call" | custom-call | tf_op jit(solution)/shard_map/tail/pallas_call | solution.py:407
Async XLA Ops:
  13.7 2.3 %collective-permute-start = (f32[16,2,128]{2,1,0:T(2,128)S(1)}, f32[16,2,128]{2,1,0:T(2,128)S(1)}, u32[]{:S(2)}, u32[]{:S(2)}) collective-permute-start(f32[16,2,128]{2,1,0:T(2,128)S(1)} %all_to_all.10.recv_ref), channel_id=1, source_target_pairs={{0,8},{8,0},{16,24},{24,16},{1,9},{9,1},{17,25},{25,17},{2,10},{10... | collective-permute-start | bytes 49160 | tf_op jit(solution)/shard_map/ppermute | solution.py:366
  16.2 8.2 %copy-start = (s32[1024,2]{0,1:T(2,128)S(1)}, s32[1024,2]{0,1:T(2,128)}, u32[]{:S(2)}) copy-start(s32[1024,2]{0,1:T(2,128)} %param.9) | copy-start | bytes 24580
  16.2 8.2 %copy-start.1 = (bf16[16,512]{1,0:T(8,128)(2,1)S(1)}, bf16[16,512]{1,0:T(8,128)(2,1)}, u32[]{:S(2)}) copy-start(bf16[16,512]{1,0:T(8,128)(2,1)} %constant.11.clone.table_ref) | copy-start | bytes 49156
